TPU v7x, 32 devices: a whole 2x2x4 slice. The times are simulated.
32 devices in a mesh: seq: 16 (over z, y, x), head: 2 (over core).
Axes of the slice: x: 2, y: 2, z: 4, core: 2. Of those that a mesh axis runs over, the one named last changes fastest.
Arguments:
- tokens: bfloat16 [8192, 2048], P('seq'), may hold values from -6 to 6
- cotangent: bfloat16 [8192, 2048], P('seq'), may hold values from -6 to 6
- lengths: int32 [4], replicated, may hold values from 1 to 7936, 8192 in all
- order: int32 [4], replicated, may hold values from 0 to 3, each once
- norm1_gain: float32 [2048], replicated, may hold values from 0.5 to 1.5
- query_weight: bfloat16 [2048, 2048], P('seq', 'head'), may hold values from -0.125 to 0.125
- key_weight: bfloat16 [2048, 2048], P('seq', 'head'), may hold values from -0.125 to 0.125
- value_weight: bfloat16 [2048, 2048], P('seq', 'head'), may hold values from -0.125 to 0.125
- beta_weight: bfloat16 [2048, 16], P('seq', 'head'), may hold values from -0.125 to 0.125
- beta_bias: float32 [16], P('head'), may hold values from -8 to 0
- conv_query: float32 [4, 2048], P(None, 'head'), may hold values from -2.5 to 2.5
- conv_key: float32 [4, 2048], P(None, 'head'), may hold values from -2.5 to 2.5
- conv_value: float32 [4, 2048], P(None, 'head'), may hold values from -2.5 to 2.5
- out_norm_gain: float32 [128], replicated, may hold values from 0.5 to 1.5
- out_weight: bfloat16 [2048, 2048], P('head', 'seq'), may hold values from -0.125 to 0.125
- norm2_gain: float32 [2048], replicated, may hold values from 0.5 to 1.5
- gate_weight: bfloat16 [2048, 5632], P('seq', 'head'), may hold values from -0.125 to 0.125
- up_weight: bfloat16 [2048, 5632], P('seq', 'head'), may hold values from -0.125 to 0.125
- down_weight: bfloat16 [5632, 2048], P('head', 'seq'), may hold values from -0.078125 to 0.078125
Outputs:
- output: bfloat16 [8192, 2048], P('seq')
- input_grad: float32 [8192, 2048], P('seq')
- norm1_gain_grad: float32 [2048], replicated
- query_weight_grad: float32 [2048, 2048], P('seq', 'head')
- key_weight_grad: float32 [2048, 2048], P('seq', 'head')
- value_weight_grad: float32 [2048, 2048], P('seq', 'head')
- beta_weight_grad: float32 [2048, 16], P('seq', 'head')
- beta_bias_grad: float32 [16], P('head')
- conv_query_grad: float32 [4, 2048], P(None, 'head')
- conv_key_grad: float32 [4, 2048], P(None, 'head')
- conv_value_grad: float32 [4, 2048], P(None, 'head')
- out_norm_gain_grad: float32 [128], replicated
- out_weight_grad: float32 [2048, 2048], P('head', 'seq')
- norm2_gain_grad: float32 [2048], replicated
- gate_weight_grad: float32 [2048, 5632], P('seq', 'head')
- up_weight_grad: float32 [2048, 5632], P('seq', 'head')
- down_weight_grad: float32 [5632, 2048], P('head', 'seq')
Inputs may be any that keep to these rules, and one draw needn't show every extreme that they name: `lengths`: they sum to 8192, and the longest has exactly 7936 tokens. `order`: each document number appears once.
All inputs are finite; a program needn't handle non-finite values.
Results may differ from a plain program's by a relative error of at most 0.01615.
Values may be sent and summed in bfloat16 or wider, within the bound.
No kernel may reach another device: no remote copies, remote signals or barrier semaphores. Data moves between devices by JAX's collectives and lax.ppermute only.
A program may use at most 320 MiB of HBM per device.

v0:
```python
import jax
import jax.numpy as jnp
from jax import lax
from jax.sharding import PartitionSpec as P

HEAD_DIM = 128
SPAN = 64


NORM_EPS = 1e-05
UNIT_EPS = 1e-06
HIGHEST = lax.Precision.HIGHEST


def from_behind(block, axis, distance):
    devices = range(lax.axis_size(axis))
    route = [(i - distance, i) for i in devices if i - distance in devices]
    return lax.ppermute(block, axis, route)


def carried_in(x, axis, combine, identity, reverse):
    length, place = (lax.axis_size(axis), lax.axis_index(axis))
    everything = jax.tree.map(lambda part: lax.all_gather(part, axis), x)
    start = jax.tree.map(
        lambda part, zero: jnp.broadcast_to(jnp.asarray(zero, part.dtype), part.shape), x, identity
    )

    def hop(k, before):
        at = length - 1 - k if reverse else k
        reached = at > place if reverse else at < place
        new = combine(before, jax.tree.map(lambda part: part[at], everything))
        return jax.tree.map(lambda a, b: jnp.where(reached, a, b), new, before)

    return lax.fori_loop(0, length, hop, start)


def rms_scale(values, gain_vector):
    return (
        values
        * lax.rsqrt(jnp.mean(values * values, axis=-1, keepdims=True) + NORM_EPS)
        * gain_vector
    )


def unit_rows(values):
    return values * lax.rsqrt(jnp.sum(values * values, axis=-1, keepdims=True) + UNIT_EPS)


def round_trip(values):
    return lax.optimization_barrier(values.astype(jnp.bfloat16)).astype(jnp.float32)


def segment_of(positions, packed):
    doc_ends = jnp.cumsum(packed)
    counted = jnp.sum((positions[:, None] >= doc_ends[None, :]).astype(jnp.int32), axis=1)
    return jnp.where(positions < 0, -1, counted)


def short_conv(padded, tap_weights, seg_padded, segment):
    row_count = segment.shape[0]
    summed = jnp.zeros((row_count, padded.shape[1]), jnp.float32)
    for offset in range(tap_weights.shape[0]):
        same_doc = (seg_padded[offset : offset + row_count] == segment)[:, None]
        summed = summed + jnp.where(
            same_doc, tap_weights[offset] * padded[offset : offset + row_count], 0.0
        )
    return jax.nn.silu(summed)


def block_masks(segment, previous):
    block_size = segment.shape[0]
    same_doc = (segment[:, None] == segment[None, :]).astype(jnp.float32)
    row_ids = lax.broadcasted_iota(jnp.int32, (block_size, block_size), 0)
    col_ids = lax.broadcasted_iota(jnp.int32, (block_size, block_size), 1)
    strict = (row_ids > col_ids).astype(jnp.float32) * same_doc
    through = (row_ids >= col_ids).astype(jnp.float32) * same_doc
    carry_in = (segment == previous).astype(jnp.float32)
    return (strict, through, carry_in)


def delta_block(carried, queries, keys_in, values_in, strength, segment, previous):
    block_size = queries.shape[1]
    strict, through, carry_in = block_masks(segment, previous)
    key_dots = jnp.einsum("hcd,hed->hce", keys_in, keys_in, precision=HIGHEST)
    system = jnp.eye(block_size, dtype=jnp.float32) + key_dots * strict * strength[:, None, :]
    right_side = values_in - carry_in[None, :, None] * jnp.einsum(
        "hcd,hde->hce", keys_in, carried, precision=HIGHEST
    )
    fresh_values = jax.scipy.linalg.solve_triangular(
        system, right_side, lower=True, unit_diagonal=True
    )
    scores = (
        jnp.einsum("hcd,hed->hce", queries, keys_in, precision=HIGHEST)
        * through
        * strength[:, None, :]
    )
    outputs = carry_in[None, :, None] * jnp.einsum(
        "hcd,hde->hce", queries, carried, precision=HIGHEST
    )
    outputs = outputs + jnp.einsum("hce,hef->hcf", scores, fresh_values, precision=HIGHEST)
    tail_weight = (segment == segment[-1]).astype(jnp.float32)[None, :] * strength
    updated = carry_in[-1] * carried + jnp.einsum(
        "hcd,hce->hde", keys_in * tail_weight[:, :, None], fresh_values, precision=HIGHEST
    )
    return (updated, outputs)


def block_map(keys_in, values_in, strength, segment, previous):
    block_size = keys_in.shape[1]
    head_size = keys_in.shape[2]
    strict, through, carry_in = block_masks(segment, previous)
    key_dots = jnp.einsum("hcd,hed->hce", keys_in, keys_in, precision=HIGHEST)
    system = jnp.eye(block_size, dtype=jnp.float32) + key_dots * strict * strength[:, None, :]
    right_side = jnp.concatenate([values_in, carry_in[None, :, None] * keys_in], axis=2)
    solved = jax.scipy.linalg.solve_triangular(system, right_side, lower=True, unit_diagonal=True)
    fresh_values = solved[:, :, :head_size]
    weighted = solved[:, :, head_size:]
    tail_weight = (segment == segment[-1]).astype(jnp.float32)[None, :] * strength
    tail_keys = keys_in * tail_weight[:, :, None]
    transition = carry_in[-1] * jnp.eye(head_size, dtype=jnp.float32) - jnp.einsum(
        "hcd,hce->hde", tail_keys, weighted, precision=HIGHEST
    )
    offset = jnp.einsum("hcd,hce->hde", tail_keys, fresh_values, precision=HIGHEST)
    return (transition, offset)


def chain_mul(first_op, second_op):
    return jnp.einsum("hde,hef->hdf", first_op, second_op, precision=HIGHEST)


def combine(earlier_map, later_map):
    return (
        chain_mul(later_map[0], earlier_map[0]),
        chain_mul(later_map[0], earlier_map[1]) + later_map[1],
    )


def body(
    tokens,
    cotangent,
    lengths,
    order,
    norm1_gain,
    query_weight,
    key_weight,
    value_weight,
    beta_weight,
    beta_bias,
    conv_query,
    conv_key,
    conv_value,
    out_norm_gain,
    out_weight,
    norm2_gain,
    gate_weight,
    up_weight,
    down_weight,
):
    row_count = tokens.shape[0]
    head_width = conv_query.shape[1]
    heads_here = head_width // HEAD_DIM
    blocks = row_count // SPAN
    tap_count = conv_query.shape[0]
    doc_ids = jnp.arange(lengths.shape[0], dtype=jnp.int32)
    packed = jnp.sum(jnp.where(order[:, None] == doc_ids[None, :], lengths[None, :], 0), axis=1)
    first_row = lax.axis_index("seq") * row_count
    segment = segment_of(first_row + jnp.arange(row_count, dtype=jnp.int32), packed)
    seg_padded = segment_of(
        first_row - (tap_count - 1) + jnp.arange(row_count + tap_count - 1, dtype=jnp.int32), packed
    )
    seg_blocks = segment.reshape(blocks, SPAN)
    prev_blocks = segment_of(first_row + SPAN * jnp.arange(blocks, dtype=jnp.int32) - 1, packed)

    def to_blocks(values):
        return values.reshape(blocks, SPAN, heads_here, HEAD_DIM).transpose(0, 2, 1, 3)

    def from_blocks(values):
        return values.transpose(0, 2, 1, 3).reshape(row_count, head_width)

    inputs = tokens.astype(jnp.float32)
    w_query, w_key, w_value, w_beta, w_out = (
        lax.all_gather(query_weight, "seq", axis=0, tiled=True),
        lax.all_gather(key_weight, "seq", axis=0, tiled=True),
        lax.all_gather(value_weight, "seq", axis=0, tiled=True),
        lax.all_gather(beta_weight, "seq", axis=0, tiled=True),
        lax.all_gather(out_weight, "seq", axis=1, tiled=True),
    )
    normed, norm1_back = jax.vjp(rms_scale, inputs, norm1_gain)
    normed_low = normed.astype(jnp.bfloat16)
    proj_query = jnp.dot(normed_low, w_query, preferred_element_type=jnp.float32).astype(
        jnp.bfloat16
    )
    proj_key = jnp.dot(normed_low, w_key, preferred_element_type=jnp.float32).astype(jnp.bfloat16)
    proj_value = jnp.dot(normed_low, w_value, preferred_element_type=jnp.float32).astype(
        jnp.bfloat16
    )
    strength = jax.nn.sigmoid(
        jnp.dot(normed_low, w_beta, preferred_element_type=jnp.float32) + beta_bias
    )
    edge = row_count - tap_count + 1
    before = from_behind((proj_query[edge:], proj_key[edge:], proj_value[edge:]), "seq", 1)
    ext_query = jnp.concatenate([before[0], proj_query], axis=0).astype(jnp.float32)
    ext_key = jnp.concatenate([before[1], proj_key], axis=0).astype(jnp.float32)
    ext_value = jnp.concatenate([before[2], proj_value], axis=0).astype(jnp.float32)

    def conv_part(padded_query, padded_key, padded_value, taps_query, taps_key, taps_value):
        conv_q = short_conv(padded_query, taps_query, seg_padded, segment)
        conv_k = short_conv(padded_key, taps_key, seg_padded, segment)
        conv_v = short_conv(padded_value, taps_value, seg_padded, segment)
        queries = unit_rows(conv_q.reshape(row_count, heads_here, HEAD_DIM)).reshape(
            row_count, head_width
        )
        keys_out = unit_rows(conv_k.reshape(row_count, heads_here, HEAD_DIM)).reshape(
            row_count, head_width
        )
        return (queries, keys_out, conv_v)

    (conv_queries, conv_keys, conv_values), conv_back = jax.vjp(
        conv_part, ext_query, ext_key, ext_value, conv_query, conv_key, conv_value
    )
    query_blocks = to_blocks(round_trip(conv_queries))
    key_blocks = to_blocks(round_trip(conv_keys))
    value_blocks = to_blocks(round_trip(conv_values))
    strength_blocks = strength.reshape(blocks, SPAN, heads_here).transpose(0, 2, 1)
    square_zero = jnp.zeros((heads_here, HEAD_DIM, HEAD_DIM), jnp.float32)
    identity_map = (
        jnp.broadcast_to(jnp.eye(HEAD_DIM, dtype=jnp.float32), (heads_here, HEAD_DIM, HEAD_DIM)),
        square_zero,
    )

    def compose(carried, inputs_in):
        return (combine(carried, block_map(*inputs_in)), None)

    (transition, offset), _ = lax.scan(
        compose, identity_map, (key_blocks, value_blocks, strength_blocks, seg_blocks, prev_blocks)
    )
    _, state_in = carried_in((transition, offset), "seq", combine, identity_map, False)

    def chain(queries, keys_in, values_in, strengths, start_state):

        def step_fn(carried, inputs_in):
            return delta_block(carried, *inputs_in)

        final_state, chain_outs = lax.scan(
            step_fn, start_state, (queries, keys_in, values_in, strengths, seg_blocks, prev_blocks)
        )
        return (chain_outs, final_state)

    (chain_outs, final_state), chain_back = jax.vjp(
        chain, query_blocks, key_blocks, value_blocks, strength_blocks, state_in
    )
    mixer_rows = from_blocks(chain_outs).reshape(row_count, heads_here, HEAD_DIM)
    out_normed, onorm_back = jax.vjp(rms_scale, mixer_rows, out_norm_gain)
    out_low = out_normed.reshape(row_count, head_width).astype(jnp.bfloat16)
    mixer_out = lax.psum(
        jnp.dot(out_low, w_out, preferred_element_type=jnp.float32).astype(jnp.bfloat16), "head"
    ).astype(jnp.float32)
    middle = inputs + mixer_out
    w_gate, w_up, w_down = (
        lax.all_gather(gate_weight, "seq", axis=0, tiled=True),
        lax.all_gather(up_weight, "seq", axis=0, tiled=True),
        lax.all_gather(down_weight, "seq", axis=1, tiled=True),
    )
    normed_two, norm2_back = jax.vjp(rms_scale, middle, norm2_gain)
    two_low = normed_two.astype(jnp.bfloat16)
    gate_part = jnp.dot(two_low, w_gate, preferred_element_type=jnp.float32)
    up_part = jnp.dot(two_low, w_up, preferred_element_type=jnp.float32)
    hidden = (jax.nn.silu(gate_part) * up_part).astype(jnp.bfloat16)
    ffn_out = lax.psum(
        jnp.dot(hidden, w_down, preferred_element_type=jnp.float32).astype(jnp.bfloat16), "head"
    ).astype(jnp.float32)
    output = (middle + ffn_out).astype(jnp.bfloat16)
    grad_hidden = jnp.dot(cotangent, w_down.T, preferred_element_type=jnp.float32)
    gate_sig = jax.nn.sigmoid(gate_part)
    grad_gate = (grad_hidden * up_part * gate_sig * (1.0 + gate_part * (1.0 - gate_sig))).astype(
        jnp.bfloat16
    )
    grad_up = (grad_hidden * gate_part * gate_sig).astype(jnp.bfloat16)
    grad_w_gate = jnp.dot(two_low.T, grad_gate, preferred_element_type=jnp.float32)
    grad_w_up = jnp.dot(two_low.T, grad_up, preferred_element_type=jnp.float32)
    grad_w_down = jnp.dot(hidden.T, cotangent, preferred_element_type=jnp.float32)
    ffn_grads = (grad_w_gate, grad_w_up, grad_w_down)
    part_two = jnp.dot(grad_gate, w_gate.T, preferred_element_type=jnp.float32) + jnp.dot(
        grad_up, w_up.T, preferred_element_type=jnp.float32
    )
    grad_normed_two = lax.psum(part_two.astype(jnp.bfloat16), "head").astype(jnp.float32)
    grad_middle_norm, grad_norm2 = norm2_back(grad_normed_two)
    grad_middle = cotangent.astype(jnp.float32) + grad_middle_norm
    grad_mix_low = grad_middle.astype(jnp.bfloat16)
    grad_w_out = jnp.dot(out_low.T, grad_mix_low, preferred_element_type=jnp.float32)
    grad_out_normed = jnp.dot(grad_mix_low, w_out.T, preferred_element_type=jnp.float32).reshape(
        row_count, heads_here, HEAD_DIM
    )
    grad_mixer_rows, grad_onorm = onorm_back(grad_out_normed)
    grad_chain = to_blocks(grad_mixer_rows.reshape(row_count, head_width))
    direct = chain_back((grad_chain, jnp.zeros_like(final_state)))
    _, state_grad = carried_in(
        (jnp.swapaxes(transition, 1, 2), direct[4]), "seq", combine, identity_map, True
    )
    carried_grads = chain_back((jnp.zeros_like(chain_outs), state_grad))
    grad_query = from_blocks(direct[0] + carried_grads[0])
    grad_key = from_blocks(direct[1] + carried_grads[1])
    grad_value = from_blocks(direct[2] + carried_grads[2])
    grad_strength = (direct[3] + carried_grads[3]).transpose(0, 2, 1).reshape(row_count, heads_here)
    grad_logit_full = grad_strength * strength * (1.0 - strength)
    grad_bias = jnp.sum(grad_logit_full, axis=0)
    grad_logit = grad_logit_full.astype(jnp.bfloat16)
    ext_grads = conv_back((grad_query, grad_key, grad_value))
    halo_rows = tap_count - 1
    after = (
        from_behind(ext_grads[0][:halo_rows].astype(jnp.bfloat16), "seq", -1).astype(jnp.float32),
        from_behind(ext_grads[1][:halo_rows].astype(jnp.bfloat16), "seq", -1).astype(jnp.float32),
        from_behind(ext_grads[2][:halo_rows].astype(jnp.bfloat16), "seq", -1).astype(jnp.float32),
    )

    def own_rows(ext_grad, extra):
        return jnp.concatenate(
            [ext_grad[halo_rows:row_count], ext_grad[row_count:] + extra], axis=0
        ).astype(jnp.bfloat16)

    grad_pq = own_rows(ext_grads[0], after[0])
    grad_pk = own_rows(ext_grads[1], after[1])
    grad_pv = own_rows(ext_grads[2], after[2])
    grad_w_query = jnp.dot(normed_low.T, grad_pq, preferred_element_type=jnp.float32)
    grad_w_key = jnp.dot(normed_low.T, grad_pk, preferred_element_type=jnp.float32)
    grad_w_value = jnp.dot(normed_low.T, grad_pv, preferred_element_type=jnp.float32)
    grad_w_beta = jnp.dot(normed_low.T, grad_logit, preferred_element_type=jnp.float32)
    part_one = jnp.dot(grad_pq, w_query.T, preferred_element_type=jnp.float32)
    part_one = part_one + jnp.dot(grad_pk, w_key.T, preferred_element_type=jnp.float32)
    part_one = part_one + jnp.dot(grad_pv, w_value.T, preferred_element_type=jnp.float32)
    part_one = part_one + jnp.dot(grad_logit, w_beta.T, preferred_element_type=jnp.float32)
    grad_normed, grad_onorm_sum = (
        lax.psum(part_one.astype(jnp.bfloat16), "head").astype(jnp.float32),
        lax.psum(grad_onorm.astype(jnp.bfloat16), "head").astype(jnp.float32),
    )
    grad_inputs_norm, grad_norm1 = norm1_back(grad_normed)
    input_grad = grad_middle + grad_inputs_norm
    every_grad = (
        lax.psum_scatter(grad_w_query, "seq", scatter_dimension=0, tiled=True),
        lax.psum_scatter(grad_w_key, "seq", scatter_dimension=0, tiled=True),
        lax.psum_scatter(grad_w_value, "seq", scatter_dimension=0, tiled=True),
        lax.psum_scatter(grad_w_beta, "seq", scatter_dimension=0, tiled=True),
        lax.psum_scatter(grad_w_out, "seq", scatter_dimension=1, tiled=True),
        lax.psum_scatter(ffn_grads[0], "seq", scatter_dimension=0, tiled=True),
        lax.psum_scatter(ffn_grads[1], "seq", scatter_dimension=0, tiled=True),
        lax.psum_scatter(ffn_grads[2], "seq", scatter_dimension=1, tiled=True),
    )
    mixer_grads = every_grad[:5]
    ffn_grads = every_grad[5:]
    small = lax.psum(
        (
            ext_grads[3],
            ext_grads[4],
            ext_grads[5],
            grad_norm1,
            grad_norm2,
            grad_onorm_sum,
            grad_bias,
        ),
        "seq",
    )
    return (
        output,
        input_grad,
        small[3],
        mixer_grads[0],
        mixer_grads[1],
        mixer_grads[2],
        mixer_grads[3],
        small[6],
        small[0],
        small[1],
        small[2],
        small[5],
        mixer_grads[4],
        small[4],
        ffn_grads[0],
        ffn_grads[1],
        ffn_grads[2],
    )


def solution(mesh):
    return jax.shard_map(
        body,
        mesh=mesh,
        in_specs=(
            P("seq", None),
            P("seq", None),
            P(),
            P(),
            P(),
            P("seq", "head"),
            P("seq", "head"),
            P("seq", "head"),
            P("seq", "head"),
            P("head"),
            P(None, "head"),
            P(None, "head"),
            P(None, "head"),
            P(),
            P("head", "seq"),
            P(),
            P("seq", "head"),
            P("seq", "head"),
            P("head", "seq"),
        ),
        out_specs=(
            P("seq", None),
            P("seq", None),
            P(),
            P("seq", "head"),
            P("seq", "head"),
            P("seq", "head"),
            P("seq", "head"),
            P("head"),
            P(None, "head"),
            P(None, "head"),
            P(None, "head"),
            P(),
            P("head", "seq"),
            P(),
            P("seq", "head"),
            P("seq", "head"),
            P("head", "seq"),
        ),
        check_vma=False,
    )
```

profile of v0, /device:TPU:10, one launch (start us, length us, event | category | flops | bytes accessed | tf_op | source)
XLA Modules:
  0.0 5542.0 jit_solution(13579376668590663718)
XLA Ops:
  45.5 42.6 all-gather.16.cloned.1.call-done
  97.0 68.5 %all-gather.18.cloned.1.call-done = bf16[2048,1024]{1,0:T(8,128)(2,1)} async-done(((bf16[128,1024]{1,0:T(8,128)(2,1)}), bf16[2048,1024]{1,0:T(8,128)(2,1)}) %all-gather.18.cloned.1.call-update) | async-done | bytes 4194320 | tf_op jit(solution)/shard_map/all_gather | solution.py:184
  190.3 420.6 %while.138 = (s32[]{:T(128)}, f32[8,128,128]{2,1,0:T(8,128)}, f32[8,128,128]{2,1,0:T(8,128)}, s32[8,64]{1,0:T(8,128)}, s32[8]{0:T(128)S(1)}, /*index=5*/f32[8,8,...) while((s32[]{:T(128)}, f32[8,128,128]{2,1,0:T(8,128)}, ...), condition=%wide.region_8.9_spmd.clone, body=%wide.region_7.8_spmd.clone.sunk | while | flops 755929920 | bytes 12894927 | solution.py:234
  636.6 84.5 %all-gather.30.cloned.1.call-done = f32[128,128,128]{2,1,0:T(8,128)} async-done(((f32[8,128,128]{2,1,0:T(8,128)}), f32[128,128,128]{2,1,0:T(8,128)}) %all-gather.30.cloned.1.call-update) | async-done | bytes 8388624 | tf_op jit(solution)/shard_map/all_gather | solution.py:23
  721.2 114.2 %all-gather.32.cloned.1.call-done = f32[128,128,128]{2,1,0:T(8,128)} async-done(((f32[8,128,128]{2,1,0:T(8,128)}), f32[128,128,128]{2,1,0:T(8,128)}) %all-gather.32.cloned.1.call-update) | async-done | bytes 8388624 | tf_op jit(solution)/shard_map/all_gather | solution.py:23
  871.4 493.4 %while.137 = (s32[]{:T(128)}, f32[8,128,128]{2,1,0:T(8,128)S(1)}, f32[8,8,64,128]{3,2,1,0:T(8,128)}, f32[8,1,64,64]{3,2,1,0:T(8,128)}, f32[8,8,1,64]{3,1,2,0:T(8...) while((s32[]{:T(128)}, f32[8,128,128]{2,1,0:T(8,128)S(1)}, ...), condition=%wide.region_13.14_spmd.clone.clone, body=%wide.region_12.13_spmd.clone.clone.sunk | while | flops 504378944 | bytes 10804277 | solution.py:244
  878.4 40.0 custom-call.41
  940.0 40.0 custom-call.41
  1001.6 40.0 custom-call.41
  1063.3 40.0 custom-call.41
  1406.4 138.3 %all-gather.24.cloned.1.call-done = bf16[2048,2816]{1,0:T(8,128)(2,1)} async-done(((bf16[128,2816]{1,0:T(8,128)(2,1)}), bf16[2048,2816]{1,0:T(8,128)(2,1)}) %all-gather.24.cloned.1.call-update) | async-done | bytes 11534352 | tf_op jit(solution)/shard_map/all_gather | solution.py:260
  1557.4 130.8 %all-gather.26.cloned.1.call-done = bf16[2048,2816]{1,0:T(8,128)(2,1)} async-done(((bf16[128,2816]{1,0:T(8,128)(2,1)}), bf16[2048,2816]{1,0:T(8,128)(2,1)}) %all-gather.26.cloned.1.call-update) | async-done | bytes 11534352 | tf_op jit(solution)/shard_map/all_gather | solution.py:261
  1700.8 170.3 %all-gather.28.cloned.1.call-done = bf16[2816,2048]{1,0:T(8,128)(2,1)} async-done(((bf16[2816,128]{1,0:T(8,128)(2,1)}), bf16[2816,2048]{1,0:T(8,128)(2,1)}) %all-gather.28.cloned.1.call-update) | async-done | bytes 11534352 | tf_op jit(solution)/shard_map/all_gather | solution.py:262
  1954.3 537.8 %while.140 = (s32[]{:T(128)}, f32[8,128,128]{2,1,0:T(8,128)S(1)}, f32[8,8,64,128]{3,1,2,0:T(8,128)}, f32[8,8,64,128]{3,1,2,0:T(8,128)}, f32[8,8,64,128]{3,2,1,0:...) while((s32[]{:T(128)}, f32[8,128,128]{2,1,0:T(8,128)S(1)}, ...), condition=%wide.region_25.27_spmd.clone, body=%wide.region_21.26_spmd.clone.sunk | while | flops 1034104896 | bytes 17584732 | solution.py:244
  2504.1 101.4 %all-gather.36.cloned.1.call-done = f32[128,128,128]{2,1,0:T(8,128)} async-done(((f32[8,128,128]{2,1,0:T(8,128)}), f32[128,128,128]{2,1,0:T(8,128)}) %all-gather.36.cloned.1.call-update) | async-done | bytes 8388624 | tf_op jit(solution)/shard_map/all_gather | solution.py:23
  2641.2 535.3 %while.136 = (s32[]{:T(128)}, f32[8,128,128]{2,1,0:T(8,128)S(1)}, f32[8,8,64,128]{3,1,2,0:T(8,128)}, f32[8,8,64,128]{3,1,2,0:T(8,128)}, f32[8,8,64,128]{3,2,1,0:...) while((s32[]{:T(128)}, f32[8,128,128]{2,1,0:T(8,128)S(1)}, ...), condition=%wide.region_32.34_spmd.clone, body=%wide.region_28.33_spmd.clone.sunk | while | flops 1033580672 | bytes 16531789 | solution.py:244
  3329.1 71.0 %all-reduce.36 = (f32[2048]{0:T(1024)}, f32[8]{0:T(128)}, f32[4,1024]{1,0:T(4,128)}, f32[4,1024]{1,0:T(4,128)}, f32[4,1024]{1,0:T(4,128)}, /*index=5*/f32[128]{0:T(128)}, f32[2048]{0:T(1024)}) all-reduce(f32[2048]{0:T(1024)S(1)} %get-tuple-element.2168, f32[8]{0:T(128)S(1)} %copy-done.118, ...), channel_id=1, replica_groups=mesh['seq'=16,'head'=2] {'seq'}, use_global_device_ids=true, to_apply=%region_38.40 | all-reduce | flops 16520 | bytes 131904 | tf_op jit(solution)/shard_map/psum | solution.py:350
  3408.1 128.9 %reduce-scatter.17.cloned.1.call-done = f32[1024,128]{1,0:T(8,128)} async-done(((f32[1024,2048]{1,0:T(8,128)}), f32[1024,128]{1,0:T(8,128)}) %reduce-scatter.17.cloned.1.call-update) | async-done | bytes 524304 | tf_op jit(solution)/shard_map/reduce_scatter | solution.py:343
  3537.1 184.2 %reduce-scatter.13.cloned.1.call-done = f32[128,1024]{1,0:T(8,128)} async-done(((f32[2048,1024]{1,0:T(8,128)}), f32[128,1024]{1,0:T(8,128)}) %reduce-scatter.13.cloned.1.call-update) | async-done | bytes 524304 | tf_op jit(solution)/shard_map/reduce_scatter | solution.py:341
  3721.2 183.0 %reduce-scatter.11.cloned.1.call-done = f32[128,1024]{1,0:T(8,128)} async-done(((f32[2048,1024]{1,0:T(8,128)}), f32[128,1024]{1,0:T(8,128)}) %reduce-scatter.11.cloned.1.call-update) | async-done | bytes 524304 | tf_op jit(solution)/shard_map/reduce_scatter | solution.py:340
  3904.2 183.1 %reduce-scatter.9.cloned.1.call-done = f32[128,1024]{1,0:T(8,128)} async-done(((f32[2048,1024]{1,0:T(8,128)}), f32[128,1024]{1,0:T(8,128)}) %reduce-scatter.9.cloned.1.call-update) | async-done | bytes 524304 | tf_op jit(solution)/shard_map/reduce_scatter | solution.py:339
  4087.4 481.9 %reduce-scatter.19.cloned.1.call-done = f32[128,2816]{1,0:T(8,128)} async-done(((f32[2048,2816]{1,0:T(8,128)}), f32[128,2816]{1,0:T(8,128)}) %reduce-scatter.19.cloned.1.call-update) | async-done | bytes 1441808 | tf_op jit(solution)/shard_map/reduce_scatter | solution.py:344
  4569.3 482.7 %reduce-scatter.21.cloned.1.call-done = f32[128,2816]{1,0:T(8,128)} async-done(((f32[2048,2816]{1,0:T(8,128)}), f32[128,2816]{1,0:T(8,128)}) %reduce-scatter.21.cloned.1.call-update) | async-done | bytes 1441808 | tf_op jit(solution)/shard_map/reduce_scatter | solution.py:345
  5052.0 482.7 %reduce-scatter.23.cloned.1.call-done = f32[2816,128]{1,0:T(8,128)} async-done(((f32[2816,2048]{1,0:T(8,128)}), f32[2816,128]{1,0:T(8,128)}) %reduce-scatter.23.cloned.1.call-update) | async-done | bytes 1441808 | tf_op jit(solution)/shard_map/reduce_scatter | solution.py:346
  (1417 shorter events, 2373.3 us)
Async XLA Ops:
  7.3 80.8 %all-gather.16.cloned.1.call-start = ((), (), s32[]{:S(2)}) async-start(), calls=%async_computation.8 | async-start | bytes 4456448 | tf_op jit(solution)/shard_map/all_gather | solution.py:183
  8.0 157.5 %all-gather.18.cloned.1.call-start = ((), (), s32[]{:S(2)}) async-start(), calls=%async_computation.9 | async-start | bytes 4456448 | tf_op jit(solution)/shard_map/all_gather | solution.py:184
  8.7 603.5 %all-gather.20.cloned.1.call-start = ((), (), s32[]{:S(2)}) async-start(), calls=%async_computation.10 | async-start | bytes 4456448 | tf_op jit(solution)/shard_map/all_gather | solution.py:182
  9.5 711.7 %all-gather.30.cloned.1.call-start = ((), (), s32[]{:S(2)}) async-start(), calls=%async_computation.25 | async-start | bytes 8912896 | tf_op jit(solution)/shard_map/all_gather | solution.py:23
  93.6 80.8 %collective-permute-start = (bf16[3,1024]{1,0:T(4,128)(2,1)S(1)}, bf16[3,1024]{1,0:T(4,128)(2,1)S(1)}, u32[]{:S(2)}, u32[]{:S(2)}) collective-permute-start(bf16[3,1024]{1,0:T(4,128)(2,1)S(1)} %slice.228), channel_id=1, source_target_pairs={{0,2},{2,4},{4,6},{6,8},{8,10},{10,12},{12,14},{14,16},{16,18},{18... | collective-permute-start | bytes 18440 | tf_op jit(solution)/shard_map/ppermute | solution.py:18
  610.9 224.5 %all-gather.32.cloned.1.call-start = ((), (), s32[]{:S(2)}) async-start(), calls=%async_computation.26 | async-start | bytes 8912896 | tf_op jit(solution)/shard_map/all_gather | solution.py:23
  611.5 761.6 %all-gather.22.cloned.1.call-start = ((), (), s32[]{:S(2)}) async-start(), calls=%async_computation.11 | async-start | bytes 4456448 | tf_op jit(solution)/shard_map/all_gather | solution.py:186
  612.1 788.4 %all-reduce.31.cloned.1.call-start = ((), (), s32[]{:S(2)}) async-start(), calls=%async_computation.12 | async-start | bytes 4194304 | tf_op jit(solution)/shard_map/psum | solution.py:255
  1379.3 165.4 %all-gather.24.cloned.1.call-start = ((), (), s32[]{:S(2)}) async-start(), calls=%async_computation.13 | async-start | bytes 12255232 | tf_op jit(solution)/shard_map/all_gather | solution.py:260
  1380.1 308.2 %all-gather.26.cloned.1.call-start = ((), (), s32[]{:S(2)}) async-start(), calls=%async_computation.14 | async-start | bytes 12255232 | tf_op jit(solution)/shard_map/all_gather | solution.py:261
  1380.8 490.4 %all-gather.28.cloned.1.call-start = ((), (), s32[]{:S(2)}) async-start(), calls=%async_computation.15 | async-start | bytes 12255232 | tf_op jit(solution)/shard_map/all_gather | solution.py:262
  1381.4 550.0 %all-reduce.33.cloned.1.call-start = ((), (), s32[]{:S(2)}) async-start(), calls=%async_computation.16 | async-start | bytes 4194304 | tf_op jit(solution)/shard_map/psum | solution.py:286
  1908.7 595.4 %all-gather.34.cloned.1.call-start = ((), (), s32[]{:S(2)}) async-start(), calls=%async_computation.27 | async-start | bytes 8912896 | tf_op jit(solution)/shard_map/all_gather | solution.py:23
  1910.7 694.7 %all-gather.36.cloned.1.call-start = ((), (), s32[]{:S(2)}) async-start(), calls=%async_computation.28 | async-start | bytes 8912896 | tf_op jit(solution)/shard_map/all_gather | solution.py:23
  2492.9 832.8 %all-reduce.35.cloned.1.call-start = ((), (), s32[]{:S(2)}) async-start(), calls=%async_computation.29 | async-start | bytes 8388608 | tf_op jit(solution)/shard_map/psum | solution.py:269
  3217.5 17.6 collective-permute-start.5
  3248.3 159.9 %reduce-scatter.15.cloned.1.call-start = ((), (), s32[]{:S(2)}) async-start(), calls=%async_computation.20 | async-start | bytes 69632 | tf_op jit(solution)/shard_map/reduce_scatter | solution.py:342
  3251.1 285.9 %reduce-scatter.17.cloned.1.call-start = ((), (), s32[]{:S(2)}) async-start(), calls=%async_computation.21 | async-start | bytes 8912896 | tf_op jit(solution)/shard_map/reduce_scatter | solution.py:343
  3261.1 460.1 %reduce-scatter.13.cloned.1.call-start = ((), (), s32[]{:S(2)}) async-start(), calls=%async_computation.19 | async-start | bytes 8912896 | tf_op jit(solution)/shard_map/reduce_scatter | solution.py:341
  3268.2 636.1 %reduce-scatter.11.cloned.1.call-start = ((), (), s32[]{:S(2)}) async-start(), calls=%async_computation.18 | async-start | bytes 8912896 | tf_op jit(solution)/shard_map/reduce_scatter | solution.py:340
  3275.6 811.7 %reduce-scatter.9.cloned.1.call-start = ((), (), s32[]{:S(2)}) async-start(), calls=%async_computation.17 | async-start | bytes 8912896 | tf_op jit(solution)/shard_map/reduce_scatter | solution.py:339
  3282.5 1286.7 %reduce-scatter.19.cloned.1.call-start = ((), (), s32[]{:S(2)}) async-start(), calls=%async_computation.22 | async-start | bytes 24510464 | tf_op jit(solution)/shard_map/reduce_scatter | solution.py:344
  3295.9 1756.1 %reduce-scatter.21.cloned.1.call-start = ((), (), s32[]{:S(2)}) async-start(), calls=%async_computation.23 | async-start | bytes 24510464 | tf_op jit(solution)/shard_map/reduce_scatter | solution.py:345
  3309.1 2225.6 %reduce-scatter.23.cloned.1.call-start = ((), (), s32[]{:S(2)}) async-start(), calls=%async_computation.24 | async-start | bytes 24510464 | tf_op jit(solution)/shard_map/reduce_scatter | solution.py:346
  (136 other events, 4247.9 us)
Sparse Core Ops, SparseCore 0:
  10.9 77.1 all-gather.15
  90.8 74.6 all-gather.17
  168.3 75.8 all-gather.19
  611.0 110.0 all-gather.29
  724.3 111.0 all-gather.31
  838.0 86.2 all-gather.21
  1379.4 21.0 all-reduce.30
  1403.6 141.0 all-gather.23
  1547.8 140.3 all-gather.25
  1691.1 179.9 all-gather.27
  1908.8 22.4 all-reduce.32
  1934.6 113.4 all-gather.33
  2493.1 112.3 all-gather.35
  3248.4 27.9 all-reduce.34
  3279.1 66.0 reduce-scatter.14
  3347.8 189.1 reduce-scatter.16
  3539.8 181.4 reduce-scatter.12
  3724.0 180.2 reduce-scatter.10
  3907.1 180.2 reduce-scatter.8
  4090.1 479.1 reduce-scatter.18
  4572.1 479.7 reduce-scatter.20
  5054.8 479.7 reduce-scatter.22
where the time goes:
time: 5560 us; the launch traced here: 5540 us
  waiting for transfers between devices  3030 us (54%)
  other arithmetic  1440 us (26%)
  matrix products  736 us (13%)
  local copies, waits for them, and re-layouts  195 us (4%)
  blocking collectives  104 us (2%)
    another operation x104, other arithmetic, delta_block(): jax.scipy.linalg.solve_triangular(system, right_side, lower=True, unit_di...  967 us
    reduce_scatter x1, waiting for transfers between devices, body(): lax.psum_scatter(ffn_grads[1], 'seq', scatter_dimension=0, tiled=True)  483 us
    reduce_scatter x1, waiting for transfers between devices, body(): lax.psum_scatter(ffn_grads[2], 'seq', scatter_dimension=1, tiled=True)  483 us
    reduce_scatter x1, waiting for transfers between devices, body(): lax.psum_scatter(ffn_grads[0], 'seq', scatter_dimension=0, tiled=True)  482 us
    another operation x32, other arithmetic, block_map(): jax.scipy.linalg.solve_triangular(system, right_side, lower=True, unit_di...  315 us
    all_gather x4, waiting for transfers between devices, carried_in(): everything = jax.tree.map(lambda part: lax.all_gather(part, axis), x)  300 us
    reduce_scatter x1, waiting for transfers between devices, body(): lax.psum_scatter(grad_w_value, 'seq', scatter_dimension=0, tiled=True)  184 us
    reduce_scatter x1, waiting for transfers between devices, body(): lax.psum_scatter(grad_w_query, 'seq', scatter_dimension=0, tiled=True)  183 us
  transfers between devices with their start and end apart: 28, of which 18 were waited for; matrix products, arithmetic and copies ran while one was open for 30% of the time, Pallas kernels for 0%

commit v1 on v0

v1 whole, which is shorter than its diff:
```python
import jax
import jax.numpy as jnp
from jax import lax
from jax.experimental import pallas as pl
from jax.experimental.pallas import tpu as pltpu
from jax.sharding import Mesh
from jax.sharding import PartitionSpec as P

HEAD_DIM = 128
CHUNK = 128
SUB = 2
NORM_EPS = 1e-05
UNIT_EPS = 1e-06
F32 = jnp.float32
BF16 = jnp.bfloat16


def mm(a, b):
    return jnp.dot(a, b, preferred_element_type=F32)


def mm_nt(a, b):
    return lax.dot_general(a, b, (((1,), (1,)), ((), ())), preferred_element_type=F32)


def mm_tn(a, b):
    return lax.dot_general(a, b, (((0,), (0,)), ((), ())), preferred_element_type=F32)


def split(a):
    high = a.astype(BF16)
    return high, (a - high.astype(F32)).astype(BF16)


def mm3(a, b):
    (ah, al), (bh, bl) = a, b
    return mm(ah, bh) + (mm(ah, bl) + mm(al, bh))


def iotas():
    rows = lax.broadcasted_iota(jnp.int32, (CHUNK, CHUNK), 0)
    cols = lax.broadcasted_iota(jnp.int32, (CHUNK, CHUNK), 1)
    return rows, cols


def inverses(systems):
    rows, cols = iotas()
    eye = (rows == cols).astype(F32)
    same8 = (rows >> 3) == (cols >> 3)
    low = [jnp.where(same8, a, 0.0) for a in systems]
    low_s = [split(n) for n in low]
    sq = [mm3(n, n) for n in low_s]
    sq_s = [split(n) for n in sq]
    first = [eye - n for n in low]
    quad = [mm3(n, n) for n in sq_s]
    t = [f + mm3(split(f), s) for f, s in zip(first, sq_s)]
    t = [x + mm3(split(x), split(n)) for x, n in zip(t, quad)]
    for level in (3, 4, 5, 6):
        joined = ((rows >> (level + 1)) == (cols >> (level + 1))) & ((rows >> level) != (cols >> level))
        off = [split(jnp.where(joined, a, 0.0)) for a in systems]
        t_s = [split(x) for x in t]
        mid = [split(mm3(o, x)) for o, x in zip(off, t_s)]
        t = [x - mm3(xs, m) for x, xs, m in zip(t, t_s, mid)]
    return t


def silu_parts(pre):
    sig = jax.nn.sigmoid(pre)
    return pre * sig, sig


def forward_one(q_ref, proj_ref, halo_ref, taps_ref, bias_ref, col_ref, row_ref,
                pre_ref, qkv_ref, beta_ref, t_ref, x_ref, last_ref, ext, state):
    step = pl.program_id(0)
    heads = state.shape[0]
    width = heads * HEAD_DIM
    rows = SUB * CHUNK
    rid, cid = iotas()

    @pl.when(step == 0)
    def _():
        ext[0:8, :] = halo_ref[:, : 3 * width].astype(F32)
        eye = (rid == cid).astype(F32)
        for h in range(heads):
            state[h, :, :CHUNK] = eye
            state[h, :, CHUNK:] = jnp.zeros((CHUNK, CHUNK), F32)

    raw = proj_ref[...]
    ext[8 : 8 + rows, :] = raw[:, : 3 * width].astype(F32)
    beta = jax.nn.sigmoid(raw[:, 3 * width :].astype(F32) + bias_ref[...])
    beta_ref[...] = beta
    col = col_ref[...]
    pre = taps_ref[3:4, :] * ext[8 : 8 + rows, :]
    for k in (1, 2, 3):
        pre = pre + taps_ref[3 - k : 4 - k, :] * (col[:, 2 + k : 3 + k] * ext[8 - k : 8 - k + rows, :])
    pre_ref[...] = pre
    tail = ext[rows : rows + 8, :]
    ext[0:8, :] = tail
    conv, _ = silu_parts(pre)
    parts = []
    for i in range(3 * heads):
        part = conv[:, i * HEAD_DIM : (i + 1) * HEAD_DIM]
        if i < 2 * heads:
            part = part * lax.rsqrt(jnp.sum(part * part, axis=1, keepdims=True) + UNIT_EPS)
        parts.append(part.astype(BF16))
        qkv_ref[:, i * HEAD_DIM : (i + 1) * HEAD_DIM] = parts[-1]

    pairs, systems = [], []
    for s in range(SUB):
        at = slice(s * CHUNK, (s + 1) * CHUNK)
        seg_row = row_ref[0:1, at]
        strict = (col[at, 0:1] == seg_row) & (rid > cid)
        beta_t = beta[at, :].T
        carry = col[at, 1:2]
        for h in range(heads):
            k = parts[heads + h][at, :]
            v = parts[2 * heads + h][at, :]
            systems.append(jnp.where(strict, mm_nt(k, k), 0.0) * beta_t[h : h + 1, :])
            kf = k.astype(F32)
            ck = (carry * kf).astype(BF16)
            kt = (col[at, 2:3] * beta[at, h : h + 1] * kf).astype(BF16)
            pairs.append((s, h, v, ck, kt, carry[CHUNK - 1 : CHUNK, :]))
    ts = inverses(systems)
    maps = []
    for (s, h, v, ck, kt, last), t in zip(pairs, ts):
        tb = t.astype(BF16)
        t_ref[h, s] = tb
        uw = mm(tb, jnp.concatenate([v, ck], axis=1)).astype(BF16)
        maps.append(mm_tn(kt, uw))
    for (s, h, v, ck, kt, last), bp in zip(pairs, maps):
        x = state[h]
        xb = x.astype(BF16)
        x_ref[h, s] = xb
        new = last * x - mm(bp[:, CHUNK:].astype(BF16), xb)
        state[h, :, :CHUNK] = new[:, :CHUNK]
        state[h, :, CHUNK:] = new[:, CHUNK:] + bp[:, :CHUNK]

    @pl.when(step == pl.num_programs(0) - 1)
    def _():
        last_ref[...] = state[...]


def forward_two(q_ref, qkv_ref, beta_ref, t_ref, x_ref, start_ref, gain_ref, col_ref, row_ref,
                low_ref, mixed_ref, s_ref, u_ref):
    heads = t_ref.shape[0]
    rid, cid = iotas()
    col = col_ref[...]
    for s in range(SUB):
        at = slice(s * CHUNK, (s + 1) * CHUNK)
        seg_row = row_ref[0:1, at]
        through = (col[at, 0:1] == seg_row) & (rid >= cid)
        beta_t = beta_ref[at, :].T
        carry = col[at, 1:2]
        for h in range(heads):
            q = qkv_ref[at, h * HEAD_DIM : (h + 1) * HEAD_DIM]
            k = qkv_ref[at, (heads + h) * HEAD_DIM : (heads + h + 1) * HEAD_DIM]
            v = qkv_ref[at, (2 * heads + h) * HEAD_DIM : (2 * heads + h + 1) * HEAD_DIM]
            x = x_ref[h, s]
            state = (mm(x[:, :CHUNK], start_ref[h].astype(BF16)) + x[:, CHUNK:].astype(F32)).astype(BF16)
            s_ref[h, s] = state
            kq = mm(jnp.concatenate([k, q], axis=0), state)
            right = (v.astype(F32) - carry * kq[:CHUNK]).astype(BF16)
            u = mm(t_ref[h, s], right).astype(BF16)
            u_ref[h, s] = u
            scores = (jnp.where(through, mm_nt(q, k), 0.0) * beta_t[h : h + 1, :]).astype(BF16)
            mixed = carry * kq[CHUNK:] + mm(scores, u)
            mixed_ref[at, h * HEAD_DIM : (h + 1) * HEAD_DIM] = mixed
            scale = lax.rsqrt(jnp.mean(mixed * mixed, axis=1, keepdims=True) + NORM_EPS)
            low_ref[at, h * HEAD_DIM : (h + 1) * HEAD_DIM] = (mixed * scale * gain_ref[...]).astype(BF16)


def backward_one(q_ref, dout_ref, mixed_ref, gain_ref, qkv_ref, beta_ref, t_ref, col_ref, row_ref,
                 do_ref, z_ref, vt_ref, y_ref, last_ref, dgain_ref, state):
    step = pl.program_id(0)
    heads = state.shape[0]
    rid, cid = iotas()

    @pl.when(step == 0)
    def _():
        eye = (rid == cid).astype(F32)
        for h in range(heads):
            state[h, :, :CHUNK] = eye
            state[h, :, CHUNK:] = jnp.zeros((CHUNK, CHUNK), F32)
        dgain_ref[...] = jnp.zeros_like(dgain_ref)

    col = col_ref[...]
    gain = gain_ref[...]
    pairs = []
    dgain = jnp.zeros((1, HEAD_DIM), F32)
    for s in reversed(range(SUB)):
        at = slice(s * CHUNK, (s + 1) * CHUNK)
        seg_row = row_ref[0:1, at]
        through_t = (col[at, 0:1] == seg_row) & (cid >= rid)
        carry = col[at, 1:2]
        for h in range(heads):
            q = qkv_ref[at, h * HEAD_DIM : (h + 1) * HEAD_DIM]
            k = qkv_ref[at, (heads + h) * HEAD_DIM : (heads + h + 1) * HEAD_DIM]
            mixed = mixed_ref[at, h * HEAD_DIM : (h + 1) * HEAD_DIM]
            dy = dout_ref[at, h * HEAD_DIM : (h + 1) * HEAD_DIM].astype(F32)
            scale = lax.rsqrt(jnp.mean(mixed * mixed, axis=1, keepdims=True) + NORM_EPS)
            normed = mixed * scale
            dgain = dgain + jnp.sum(dy * normed, axis=0, keepdims=True)
            gdy = gain * dy
            do = (scale * (gdy - normed * jnp.mean(normed * gdy, axis=1, keepdims=True))).astype(BF16)
            do_ref[at, h * HEAD_DIM : (h + 1) * HEAD_DIM] = do
            beta = beta_ref[at, h : h + 1]
            scores_t = (jnp.where(through_t, mm_nt(k, q), 0.0) * beta).astype(BF16)
            kf = k.astype(F32)
            kt = (col[at, 2:3] * beta * kf).astype(BF16)
            ck = (carry * kf).astype(BF16)
            cq = (carry * q.astype(F32)).astype(BF16)
            md = mm(scores_t, do).astype(BF16)
            zv = mm_tn(t_ref[h, s], jnp.concatenate([md, kt], axis=1))
            z_ref[h, s] = zv[:, :CHUNK]
            zvb = zv.astype(BF16)
            vt_ref[h, s] = zvb[:, CHUNK:]
            dp = mm_tn(ck, zvb)
            d = mm_tn(cq, do) - dp[:, :CHUNK]
            pairs.append((s, h, d, dp[:, CHUNK:].astype(BF16), carry[CHUNK - 1 : CHUNK, :]))
    dgain_ref[...] += dgain
    for s, h, d, p, last in pairs:
        y = state[h]
        yb = y.astype(BF16)
        y_ref[h, s] = yb
        new = last * y - mm(p, yb)
        state[h, :, :CHUNK] = new[:, :CHUNK]
        state[h, :, CHUNK:] = new[:, CHUNK:] + d

    @pl.when(step == pl.num_programs(0) - 1)
    def _():
        last_ref[...] = state[...]


def backward_two(q_ref, pre_ref, proj_ref, taps_ref, qkv_ref, beta_ref, do_ref, z_ref, vt_ref, y_ref, s_ref, u_ref,
                 end_ref, col_ref, row_ref,
                 dproj_ref, head_ref, dtaps_ref, dbias_ref, ext):
    step = pl.program_id(0)
    heads = z_ref.shape[0]
    width = heads * HEAD_DIM
    rows = SUB * CHUNK
    rid, cid = iotas()

    @pl.when(step == 0)
    def _():
        ext[rows : rows + 8, :] = jnp.zeros((8, 3 * width), F32)
        dtaps_ref[...] = jnp.zeros_like(dtaps_ref)
        dbias_ref[...] = jnp.zeros_like(dbias_ref)

    col = col_ref[...]
    lane = lax.broadcasted_iota(jnp.int32, (CHUNK, 128), 1)
    dbias = jnp.zeros((1, 128), F32)
    for s in range(SUB):
        at = slice(s * CHUNK, (s + 1) * CHUNK)
        seg_row = row_ref[0:1, at]
        same = col[at, 0:1] == seg_row
        through_t = same & (cid >= rid)
        strict_t = same & (cid > rid)
        carry = col[at, 1:2]
        tail = col[at, 2:3]
        dlog = jnp.zeros((CHUNK, 128), F32)
        for h in range(heads):
            q = qkv_ref[at, h * HEAD_DIM : (h + 1) * HEAD_DIM]
            k = qkv_ref[at, (heads + h) * HEAD_DIM : (heads + h + 1) * HEAD_DIM]
            do = do_ref[at, h * HEAD_DIM : (h + 1) * HEAD_DIM]
            beta = beta_ref[at, h : h + 1]
            state = s_ref[h, s]
            u = u_ref[h, s]
            y = y_ref[h, s]
            g = (mm(y[:, :CHUNK], end_ref[h].astype(BF16)) + y[:, CHUNK:].astype(F32)).astype(BF16)
            dr = z_ref[h, s] + mm(vt_ref[h, s], g)
            drb = dr.astype(BF16)
            kk = mm_nt(k, k)
            kq = mm_nt(k, q)
            dm_t = jnp.where(through_t, mm_nt(u, do), 0.0)
            da_t = jnp.where(strict_t, -mm_nt(u, drb), 0.0)
            ug = mm_nt(u, g)
            kf = k.astype(F32)
            dbeta = jnp.sum(dm_t * kq + da_t * kk + tail * (kf * ug), axis=1, keepdims=True)
            dqk_t = (dm_t * beta).astype(BF16)
            dkk_t = da_t * beta
            dkk = (dkk_t + dkk_t.T).astype(BF16)
            sd = mm_nt(jnp.concatenate([do, drb], axis=0), state)
            dq = carry * sd[:CHUNK] + mm_tn(dqk_t, k)
            dk = mm(dqk_t, q) + mm(dkk, k) + (tail * beta) * ug - carry * sd[CHUNK:]
            dl = dbeta * beta * (1.0 - beta)
            dlog = jnp.where(lane == h, dl, dlog)
            qf = q.astype(F32)
            for i, d, unit in ((h, dq, qf), (heads + h, dk, kf), (2 * heads + h, dr, None)):
                lanes = slice(i * HEAD_DIM, (i + 1) * HEAD_DIM)
                pre = pre_ref[at, lanes]
                conv, sig = silu_parts(pre)
                if unit is not None:
                    scale = lax.rsqrt(jnp.sum(conv * conv, axis=1, keepdims=True) + UNIT_EPS)
                    d = (d - unit * jnp.sum(unit * d, axis=1, keepdims=True)) * scale
                ext[at, lanes] = d * (sig * (1.0 + pre * (1.0 - sig)))
        dproj_ref[at, 3 * width :] = dlog.astype(BF16)
        dbias = dbias + jnp.sum(dlog, axis=0, keepdims=True)
    dbias_ref[...] += dbias
    proj = proj_ref[:, : 3 * width].astype(F32)
    total = taps_ref[3:4, :] * ext[0:rows, :]
    dtaps_ref[3:4, :] += jnp.sum(proj * ext[0:rows, :], axis=0, keepdims=True)
    for k in (1, 2, 3):
        moved = col[:, 5 + k : 6 + k] * ext[k : k + rows, :]
        total = total + taps_ref[3 - k : 4 - k, :] * moved
        dtaps_ref[3 - k : 4 - k, :] += jnp.sum(proj * moved, axis=0, keepdims=True)
    dproj_ref[:, : 3 * width] = total.astype(BF16)
    first = ext[0:8, :]
    ext[rows : rows + 8, :] = first

    @pl.when(step == pl.num_programs(0) - 1)
    def _():
        head_ref[...] = first


def call(body, q, ins, outs, scratch, rows, chip_rows, reverse, flops, name):
    steps = rows // (SUB * CHUNK)
    per_chip = chip_rows // (SUB * CHUNK)

    def at(i):
        return steps - 1 - i if reverse else i

    def spec(shape, kind):
        if kind == "seq":
            return pl.BlockSpec((SUB * CHUNK, shape[1]), lambda i, qr: (at(i), 0))
        if kind == "rel":
            return pl.BlockSpec(
                (SUB * CHUNK, shape[1]),
                lambda i, qr: (((at(i) // per_chip) ^ qr[0]) * per_chip + at(i) % per_chip, 0),
            )
        if kind == "lane":
            return pl.BlockSpec((shape[0], SUB * CHUNK), lambda i, qr: (0, at(i)))
        if kind == "blk":
            return pl.BlockSpec((shape[0], SUB) + shape[2:], lambda i, qr: (0, at(i), 0, 0))
        return pl.BlockSpec(shape, lambda i, qr: (0,) * len(shape))

    nbytes = sum(a.size * a.dtype.itemsize for a, _ in ins) + sum(a.size * a.dtype.itemsize for a, _ in outs)
    return pl.pallas_call(
        body,
        grid_spec=pltpu.PrefetchScalarGridSpec(
            num_scalar_prefetch=1,
            grid=(steps,),
            in_specs=[spec(a.shape, kind) for a, kind in ins],
            out_specs=[spec(a.shape, kind) for a, kind in outs],
            scratch_shapes=scratch,
        ),
        out_shape=[a for a, _ in outs],
        compiler_params=pltpu.CompilerParams(
            dimension_semantics=("arbitrary",), vmem_limit_bytes=48 * 1024 * 1024
        ),
        cost_estimate=pl.CostEstimate(flops=flops, bytes_accessed=nbytes, transcendentals=0),
        name=name,
    )(q, *[a for a, _ in ins])


def shape(dims, dtype):
    return jax.ShapeDtypeStruct(dims, dtype)


def mixer_forward_one(q, proj, halo, taps, bias, cols, lanes, chip_rows):
    rows = proj.shape[0]
    width = taps.shape[1]
    heads = width // (3 * HEAD_DIM)
    n = rows // CHUNK
    return call(
        forward_one, q,
        [(proj, "rel"), (halo, "all"), (taps, "all"), (bias, "all"), (cols, "seq"), (lanes, "lane")],
        [(shape((rows, width), F32), "seq"), (shape((rows, width), BF16), "seq"), (shape((rows, 128), F32), "seq"),
         (shape((heads, n, CHUNK, CHUNK), BF16), "blk"), (shape((heads, n, CHUNK, 2 * CHUNK), BF16), "blk"),
         (shape((heads, CHUNK, 2 * CHUNK), F32), "all")],
        [pltpu.VMEM((SUB * CHUNK + 8, width), F32), pltpu.VMEM((heads, CHUNK, 2 * CHUNK), F32)],
        rows, chip_rows, False, 2 * heads * n * 50 * CHUNK**3, "delta_forward_one")


def mixer_forward_two(q, qkv, beta, t, x, start, gain, cols, lanes, chip_rows):
    rows = qkv.shape[0]
    heads, n = t.shape[:2]
    return call(
        forward_two, q,
        [(qkv, "seq"), (beta, "seq"), (t, "blk"), (x, "blk"), (start, "all"), (gain, "all"), (cols, "seq"), (lanes, "lane")],
        [(shape((rows, heads * HEAD_DIM), BF16), "rel"), (shape((rows, heads * HEAD_DIM), F32), "seq"),
         (shape((heads, n, CHUNK, CHUNK), BF16), "blk"), (shape((heads, n, CHUNK, CHUNK), BF16), "blk")],
        [], rows, chip_rows, False, 2 * heads * n * 8 * CHUNK**3, "delta_forward_two")


def mixer_backward_one(q, dout, mixed, gain, qkv, beta, t, cols, lanes, chip_rows):
    rows = qkv.shape[0]
    heads, n = t.shape[:2]
    return call(
        backward_one, q,
        [(dout, "rel"), (mixed, "seq"), (gain, "all"), (qkv, "seq"), (beta, "seq"), (t, "blk"), (cols, "seq"), (lanes, "lane")],
        [(shape((rows, heads * HEAD_DIM), BF16), "seq"), (shape((heads, n, CHUNK, CHUNK), F32), "blk"),
         (shape((heads, n, CHUNK, CHUNK), BF16), "blk"), (shape((heads, n, CHUNK, 2 * CHUNK), BF16), "blk"),
         (shape((heads, CHUNK, 2 * CHUNK), F32), "all"), (shape((1, HEAD_DIM), F32), "all")],
        [pltpu.VMEM((heads, CHUNK, 2 * CHUNK), F32)],
        rows, chip_rows, True, 2 * heads * n * 12 * CHUNK**3, "delta_backward_one")


def mixer_backward_two(q, pre, proj, taps, qkv, beta, do, z, vt, y, s, u, end, cols, lanes, chip_rows):
    rows, width = pre.shape
    heads, n = z.shape[:2]
    return call(
        backward_two, q,
        [(pre, "seq"), (proj, "rel"), (taps, "all"), (qkv, "seq"), (beta, "seq"), (do, "seq"), (z, "blk"), (vt, "blk"),
         (y, "blk"), (s, "blk"), (u, "blk"), (end, "all"), (cols, "seq"), (lanes, "lane")],
        [(shape((rows, width + 128), BF16), "rel"), (shape((8, width), F32), "all"), (shape((4, width), F32), "all"),
         (shape((1, 128), F32), "all")],
        [pltpu.VMEM((SUB * CHUNK + 8, width), F32)],
        rows, chip_rows, True, 2 * heads * n * 14 * CHUNK**3, "delta_backward_two")


PLANE = 4
SWAP = [(0, 1), (1, 0)]
DIAGONAL = [(0, 3), (1, 2), (2, 1), (3, 0)]
PAD = 128


def send(block, axis):
    return lax.ppermute(block, axis, DIAGONAL if axis == ("y", "x") else SWAP)


def along(block, step):
    n = lax.axis_size("z")
    return lax.ppermute(block, "z", [(i, i + step) for i in range(n) if 0 <= i + step < n])


def gather_rows(block):
    half = block.shape[0] // 2
    from_x = send(block, "x")
    from_y = send(block, "y")
    far_top = send(from_y[:half], "x")
    far_low = send(from_x[half:], "y")
    return [block, from_x, from_y, far_top, far_low]


def widen(pieces, head):
    rows = []
    for piece in pieces:
        other = send(piece, "head")
        rows.append(
            jnp.where(head == 0, jnp.concatenate([piece, other], 1), jnp.concatenate([other, piece], 1))
        )
    return jnp.concatenate(rows, 0)


def scatter_rows(part):
    size = part.shape[0] // PLANE
    half = size // 2
    own, at_x, at_y, far = (part[i * size : (i + 1) * size] for i in range(PLANE))
    top = send(far[:half], "x")
    low = send(far[half:], "y")
    at_y = jnp.concatenate([(at_y[:half].astype(F32) + top.astype(F32)).astype(BF16), at_y[half:]], 0)
    at_x = jnp.concatenate([at_x[:half], (at_x[half:].astype(F32) + low.astype(F32)).astype(BF16)], 0)
    from_x = send(at_x, "x")
    from_y = send(at_y, "y")
    return own.astype(F32) + from_x.astype(F32) + from_y.astype(F32)


def half_of(array, head, axis):
    size = array.shape[axis] // 2
    return lax.dynamic_slice_in_dim(array, head * size, size, axis)


def reduce_cores(left, right_rows, head):
    other = mm_nt(left, half_of(right_rows, 1 - head, 0)).astype(BF16)
    own = mm_nt(left, half_of(right_rows, head, 0))
    return (own + send(other, "head").astype(F32)).astype(BF16)


def in_order(pieces, place):
    result = []
    for i in range(PLANE):
        out = pieces[i]
        for j in range(PLANE):
            if j != i:
                out = jnp.where(place == (i ^ j), pieces[j], out)
        result.append(out)
    return result


def exchange(pieces):
    return [pieces[0], send(pieces[1], "x"), send(pieces[2], "y"), send(pieces[3], ("y", "x"))]


def row_sum(values):
    own = jnp.sum(values, axis=1)
    return (own + send(own, "head"))[:, None]


def everywhere(values):
    for axis in ("x", "y"):
        values = values + send(values, axis)
    n = lax.axis_size("z")
    step = 1
    while step < n:
        values = values + lax.ppermute(values, "z", [(i, i ^ step) for i in range(n)])
        step *= 2
    return values


def segment_of(positions, doc_ends):
    counted = jnp.sum((positions[..., None] >= doc_ends).astype(jnp.int32), axis=-1)
    return jnp.where(positions < 0, -1, counted)


def mask_arrays(first, rows, doc_ends):
    def seg_at(offset):
        return segment_of(first + offset + jnp.arange(rows, dtype=jnp.int32), doc_ends)

    places = jnp.arange(rows, dtype=jnp.int32)
    starts = (places // CHUNK) * CHUNK
    own = seg_at(0)
    before = segment_of(first + starts - 1, doc_ends)
    last = segment_of(first + starts + CHUNK - 1, doc_ends)
    columns = [own, own == before, own == last]
    columns += [seg_at(-k) == own for k in (1, 2, 3)] + [seg_at(k) == own for k in (1, 2, 3)]
    columns = jnp.stack([c.astype(F32) for c in columns] + [jnp.zeros((rows,), F32)] * 7, axis=1)
    lanes = jnp.concatenate([own.astype(F32)[None], jnp.zeros((7, rows), F32)], 0)
    return columns, lanes


def ff_starts(total, place):
    tiles = total // 128
    base, extra = tiles // PLANE, tiles % PLANE
    most = base + (1 if extra else 0)
    start = (place * base + jnp.minimum(place, extra)) * 128
    own = (base + (place < extra).astype(jnp.int32)) * 128
    sizes = [(base + (1 if i < extra else 0)) * 128 for i in range(PLANE)]
    return start, own, most * 128, sizes


def body(
    tokens,
    cotangent,
    lengths,
    order,
    norm1_gain,
    query_weight,
    key_weight,
    value_weight,
    beta_weight,
    beta_bias,
    conv_query,
    conv_key,
    conv_value,
    out_norm_gain,
    out_weight,
    norm2_gain,
    gate_weight,
    up_weight,
    down_weight,
):
    chip_rows, model = tokens.shape
    depth = query_weight.shape[0]
    units = gate_weight.shape[1]
    rows = PLANE * chip_rows
    half = model // 2
    heads = beta_weight.shape[1] // PLANE
    width = heads * HEAD_DIM
    head = lax.axis_index("head")
    z = lax.axis_index("z")
    place = 2 * lax.axis_index("y") + lax.axis_index("x")
    place_array = jnp.reshape(place, (1,)).astype(jnp.int32)

    doc_ids = jnp.arange(lengths.shape[0], dtype=jnp.int32)
    packed = jnp.sum(jnp.where(order[:, None] == doc_ids[None, :], lengths[None, :], 0), axis=1)
    doc_ends = jnp.cumsum(packed)
    columns, lanes = mask_arrays(z * rows, rows, doc_ends)

    def mixer_piece(j):
        to = place ^ j
        parts = [
            lax.dynamic_slice_in_dim(w, to * width, width, 1) for w in (query_weight, key_weight, value_weight)
        ]
        beta = lax.dynamic_slice_in_dim(beta_weight, to * heads, heads, 1)
        return jnp.concatenate(parts + [jnp.pad(beta, ((0, 0), (0, 128 - heads)))], 1)

    def gather_weight(pieces):
        return lax.all_gather(jnp.concatenate(in_order(exchange(pieces), place), 0), "z", axis=0, tiled=True)

    w_mix = gather_weight([mixer_piece(j) for j in range(PLANE)])
    inputs = tokens.astype(F32)
    scale_one = lax.rsqrt(jnp.mean(inputs * inputs, axis=1, keepdims=True) + NORM_EPS)
    normed_half = half_of((inputs * scale_one * norm1_gain).astype(BF16), head, 1)
    x_one = widen(gather_rows(normed_half), head)
    out_rows = out_weight.T
    w_out = gather_weight(
        [lax.dynamic_slice_in_dim(out_rows, (place ^ j) * width, width, 1) for j in range(PLANE)]
    )
    ff_sizes = ff_starts(units, place)[3]

    def ff_piece(weights, j):
        start, own, most, _ = ff_starts(units, place ^ j)
        parts = []
        for w in weights:
            cut = lax.dynamic_slice_in_dim(jnp.pad(w, ((0, 0), (0, PAD))), start, most, 1)
            parts.append(jnp.where(lax.broadcasted_iota(jnp.int32, cut.shape, 1) < own, cut, 0))
        return jnp.concatenate(parts, 1)

    w_gu = gather_weight([ff_piece((gate_weight, up_weight), j) for j in range(PLANE)])
    down_rows = down_weight.T
    w_down = gather_weight([ff_piece((down_rows,), j) for j in range(PLANE)])
    dy = widen(gather_rows(half_of(cotangent, head, 1)), head)

    proj = mm(x_one, w_mix).astype(BF16)
    place_last = (PLANE - 1) ^ place
    tail_rows = lax.dynamic_slice_in_dim(proj, (place_last + 1) * chip_rows - 8, 8, 0)
    halo = along(tail_rows, 1)
    my_columns = [lax.dynamic_slice_in_dim(t, place * width, width, 1) for t in (conv_query, conv_key, conv_value)]
    taps = jnp.concatenate(my_columns, 1)
    bias = jnp.pad(lax.dynamic_slice_in_dim(beta_bias, place * heads, heads, 0), (0, 128 - heads))[None]
    gain_out = out_norm_gain[None]
    pre, qkv, beta, t, prefix, last = mixer_forward_one(
        place_array, proj, halo, taps, bias, columns, lanes, chip_rows
    )

    def chain(maps, step):
        start = jnp.zeros((heads, HEAD_DIM, HEAD_DIM), F32)
        for _ in range(lax.axis_size("z") - 1):
            moved = jnp.einsum("hij,hjk->hik", maps[:, :, :HEAD_DIM], start, precision=lax.Precision.HIGHEST)
            start = along(moved + maps[:, :, HEAD_DIM:], step)
        return start

    state_in = chain(last, 1)
    out_low, mixed, states, fresh = mixer_forward_two(
        place_array, qkv, beta, t, prefix, state_in, gain_out, columns, lanes, chip_rows
    )
    middle = half_of(inputs, head, 1) + scatter_rows(reduce_cores(out_low, w_out, head))

    gain_two = half_of(norm2_gain, head, 0)
    scale_two = lax.rsqrt(row_sum(middle * middle) / model + NORM_EPS)
    x_two = widen(gather_rows((middle * scale_two * gain_two).astype(BF16)), head)
    wide = w_down.shape[1]
    gate_up = mm(x_two, w_gu)
    gate, up = gate_up[:, :wide], gate_up[:, wide:]
    dhidden = mm(dy, w_down)
    sig = jax.nn.sigmoid(gate)
    hidden = (gate * sig * up).astype(BF16)
    dgate = (dhidden * up * sig * (1.0 + gate * (1.0 - sig))).astype(BF16)
    dup = (dhidden * gate * sig).astype(BF16)
    dgu = jnp.concatenate([dgate, dup], 1)
    dnormed_two = scatter_rows(reduce_cores(dgu, w_gu, head))

    def scatter_weight(grad):
        return lax.psum_scatter(grad.astype(BF16), "z", scatter_dimension=0, tiled=True)

    def return_weight(grad):
        pieces = [lax.dynamic_slice_in_dim(grad, (place ^ j) * depth, depth, 0) for j in range(PLANE)]
        return in_order(exchange(pieces), place)

    grad_gu = scatter_weight(mm_tn(x_two, dgu))
    grad_down = scatter_weight(mm_tn(dy, hidden))
    ffn_out = scatter_rows(reduce_cores(hidden, w_down, head))
    output_half = (middle + ffn_out).astype(BF16)

    normed_mid = middle * scale_two
    gdy = dnormed_two * gain_two
    dmiddle = half_of(cotangent, head, 1).astype(F32) + scale_two * (
        gdy - normed_mid * (row_sum(normed_mid * gdy) / model)
    )
    grad_norm2 = jnp.sum(dnormed_two * normed_mid, axis=0)
    dmix = widen(gather_rows(dmiddle.astype(BF16)), head)

    dout = mm(dmix, w_out)
    grad_out = scatter_weight(mm_tn(dmix, out_low))
    do, zed, vt, suffix, first, grad_onorm = mixer_backward_one(
        place_array, dout, mixed, gain_out, qkv, beta, t, columns, lanes, chip_rows
    )
    state_end = chain(first, -1)
    dproj, da_head, grad_taps, grad_bias = mixer_backward_two(
        place_array, pre, proj, taps, qkv, beta, do, zed, vt, suffix, states, fresh, state_end, columns, lanes, chip_rows
    )
    da_next = along(da_head, -1)
    tail_at = (place_last + 1) * chip_rows - 8
    tail_proj = lax.dynamic_slice_in_dim(proj, tail_at, 8, 0)[:, : 3 * width].astype(F32)
    places = z * rows + rows - 8 + jnp.arange(8, dtype=jnp.int32)
    own_seg = segment_of(places, doc_ends)
    extra = jnp.zeros((8, 3 * width), F32)
    extra_taps = [jnp.zeros((3 * width,), F32)]
    for k in (1, 2, 3):
        same = (segment_of(places + k, doc_ends) == own_seg) & (jnp.arange(8) + k >= 8)
        moved = jnp.where(same[:, None], jnp.concatenate([jnp.zeros((8 - k, 3 * width), F32), da_next[:k]], 0), 0.0)
        extra = extra + taps[3 - k] * moved
        extra_taps.insert(0, jnp.sum(tail_proj * moved, axis=0))
    grad_taps = grad_taps + jnp.stack(extra_taps)
    tail_old = lax.dynamic_slice_in_dim(dproj, tail_at, 8, 0)
    tail_new = (tail_old.astype(F32) + jnp.pad(extra, ((0, 0), (0, 128)))).astype(BF16)
    dproj = lax.dynamic_update_slice_in_dim(dproj, tail_new, tail_at, 0)

    grad_mix = scatter_weight(mm_tn(x_one, dproj))
    dnormed_one = scatter_rows(reduce_cores(dproj, w_mix, head))
    inputs_half = half_of(inputs, head, 1)
    normed_in = inputs_half * scale_one
    gdy = dnormed_one * half_of(norm1_gain, head, 0)
    input_half = dmiddle + scale_one * (gdy - normed_in * (row_sum(normed_in * gdy) / model))
    grad_norm1 = jnp.sum(dnormed_one * normed_in, axis=0)

    small_taps = jnp.zeros((PLANE, 4, 3 * width), F32)
    small_taps = lax.dynamic_update_slice(small_taps, grad_taps[None], (place, 0, 0))
    small_bias = jnp.zeros((PLANE, 128), F32)
    small_bias = lax.dynamic_update_slice(small_bias, grad_bias, (place, 0))
    flat = jnp.concatenate(
        [
            small_taps.reshape(-1, 128),
            small_bias,
            grad_onorm,
            jnp.zeros((3, 128), F32),
            grad_norm1.reshape(-1, 128),
            grad_norm2.reshape(-1, 128),
        ],
        0,
    )
    flat = everywhere(flat)
    cut = PLANE * 12 * width // 128
    taps_sum = flat[:cut].reshape(PLANE, 4, 3, width)
    taps_sum = taps_sum.transpose(2, 1, 0, 3).reshape(3, 4, PLANE * width)
    bias_sum = flat[cut : cut + PLANE, :heads].reshape(-1)
    shared = flat[cut + PLANE :]
    shared_other = send(shared, "head")
    onorm_sum = shared[0] + shared_other[0]
    per = half // 128

    def both(own, other):
        own, other = own.reshape(-1), other.reshape(-1)
        return jnp.where(head == 0, jnp.concatenate([own, other]), jnp.concatenate([other, own]))

    norm1_sum = both(shared[4 : 4 + per], shared_other[4 : 4 + per])
    norm2_sum = both(shared[4 + per :], shared_other[4 + per :])

    mix_home = return_weight(grad_mix)
    out_home = return_weight(grad_out)
    gu_home = return_weight(grad_gu)
    down_home = return_weight(grad_down)

    def columns_of(home, start, sizes):
        return jnp.concatenate([p[:, start : start + s] for p, s in zip(home, sizes)], 1).astype(F32)

    even = [width] * PLANE
    output = widen([output_half], head)
    input_grad = widen([input_half], head)
    return (
        output,
        input_grad,
        norm1_sum,
        columns_of(mix_home, 0, even),
        columns_of(mix_home, width, even),
        columns_of(mix_home, 2 * width, even),
        columns_of(mix_home, 3 * width, [heads] * PLANE),
        bias_sum,
        taps_sum[0],
        taps_sum[1],
        taps_sum[2],
        onorm_sum,
        columns_of(out_home, 0, even).T,
        norm2_sum,
        columns_of(gu_home, 0, ff_sizes),
        columns_of(gu_home, wide, ff_sizes),
        columns_of(down_home, 0, ff_sizes).T,
    )


def solution(mesh):
    planes = mesh.shape["seq"] // PLANE
    grid = Mesh(mesh.devices.reshape(planes, 2, 2, 2), ("z", "y", "x", "head"))
    seq = ("z", "y", "x")
    return jax.shard_map(
        body,
        mesh=grid,
        in_specs=(
            P(seq, None),
            P(seq, None),
            P(),
            P(),
            P(),
            P(seq, "head"),
            P(seq, "head"),
            P(seq, "head"),
            P(seq, "head"),
            P("head"),
            P(None, "head"),
            P(None, "head"),
            P(None, "head"),
            P(),
            P("head", seq),
            P(),
            P(seq, "head"),
            P(seq, "head"),
            P("head", seq),
        ),
        out_specs=(
            P(seq, None),
            P(seq, None),
            P(),
            P(seq, "head"),
            P(seq, "head"),
            P(seq, "head"),
            P(seq, "head"),
            P("head"),
            P(None, "head"),
            P(None, "head"),
            P(None, "head"),
            P(),
            P("head", seq),
            P(),
            P(seq, "head"),
            P(seq, "head"),
            P("head", seq),
        ),
        check_vma=False,
    )
```

time: 5560 us -> 907 us (0.16)
  waiting for transfers between devices: 3030 us -> 338 us
  other arithmetic: 1440 us -> 118 us
  matrix products: 736 us -> 158 us
  local copies, waits for them, and re-layouts: 195 us -> 76.3 us
  blocking collectives: 104 us -> 0 us
  Pallas kernels: 0 us -> 92.2 us
  starting transfers between devices: 21.7 us -> 98.5 us
    reduce_scatter x8 -> x4, waiting for transfers between devices: 2130 us -> 0.03 us  [scatter_weight(): lax.psum_scatter(grad.astype(BF16), 'z', scatter_dimension=0, tiled=True)]
    another operation x152 -> x1, other arithmetic: 1300 us -> 0.18 us  [the longest x104 967 us: delta_block(): jax.scipy.linalg.solve_triangular(system, right_side, lower=True, unit_di...]
    all_gather x11 -> x4, waiting for transfers between devices: 851 us -> 0.01 us  [gather_weight(): lax.all_gather(jnp.concatenate(in_order(exchange(pieces), place), 0), 'z'...]
    dot_general x352 -> x22, matrix products: 673 us -> 158 us  [the longest x4 57.2 us: mm(): return jnp.dot(a, b, preferred_element_type=F32)]
    ppermute x6 -> x98, waiting for transfers between devices: 2.93 us -> 338 us  [the longest x88 282 us: send(): return lax.ppermute(block, axis, DIAGONAL if axis == ('y', 'x') else SWAP)]
    pallas_call x0 -> x4, Pallas kernels: none -> 92.2 us  [call(): pl.pallas_call(body, grid_spec=pltpu.PrefetchScalarGridSpec(num_scalar_pr...]
    ppermute x6 -> x98, starting transfers between devices: 20.3 us -> 97.9 us  [the longest x88 72.6 us: send(): return lax.ppermute(block, axis, DIAGONAL if axis == ('y', 'x') else SWAP)]
    psum x2 -> x0, blocking collectives: 73.5 us -> none  [the longest x1 71 us: body(): lax.psum((ext_grads[3], ext_grads[4], ext_grads[5], grad_norm1, grad_norm...]
  transfers between devices with their start and end apart: 28 -> 106, of which waited for: 18 -> 52; matrix products, arithmetic and copies ran while one was open for 30% -> 32% of each run, Pallas kernels for 0% -> 10%
where the time goes in v1:
time: 907 us; the launch traced here: 897 us
  waiting for transfers between devices  338 us (37%)
  matrix products  158 us (17%)
  other arithmetic  118 us (13%)
  starting transfers between devices  98.5 us (11%)
  Pallas kernels  92.2 us (10%)
  local copies, waits for them, and re-layouts  76.3 us (8%)
  between operations  15.9 us (2%)
    ppermute x88, waiting for transfers between devices, send(): return lax.ppermute(block, axis, DIAGONAL if axis == ('y', 'x') else SWAP)  282 us
    pallas_call x4, Pallas kernels, call(): pl.pallas_call(body, grid_spec=pltpu.PrefetchScalarGridSpec(num_scalar_pr...  92.2 us
    ppermute x88, starting transfers between devices, send(): return lax.ppermute(block, axis, DIAGONAL if axis == ('y', 'x') else SWAP)  72.6 us
    dot_general x4, matrix products, mm(): return jnp.dot(a, b, preferred_element_type=F32)  57.2 us
    dot_general x8, matrix products, mm_nt(): lax.dot_general(a, b, (((1,), (1,)), ((), ())), preferred_element_type=F32)  53 us
    ppermute x8, waiting for transfers between devices, along(): lax.ppermute(block, 'z', [(i, i + step) for i in range(n) if 0 <= i + ste...  51.3 us
    dot_general x4, matrix products, mm_tn(): lax.dot_general(a, b, (((0,), (0,)), ((), ())), preferred_element_type=F32)  46 us
    unnamed x140, local copies, waits for them, and re-layouts  44.2 us
  transfers between devices with their start and end apart: 106, of which 52 were waited for; matrix products, arithmetic and copies ran while one was open for 32% of the time, Pallas kernels for 10%

profile of v1, /device:TPU:10, one launch (start us, length us, event | category | flops | bytes accessed | tf_op | source)
XLA Modules:
  0.0 896.7 jit_solution(17141519179886005760)
XLA Ops:
  57.0 10.2 %collective-permute-done.1 = bf16[512,1024]{0,1:T(8,128)(2,1)} collective-permute-done((bf16[512,1024]{0,1:T(8,128)(2,1)}, bf16[512,1024]{0,1:T(8,128)(2,1)}, u32[]{:S(2)}, u32[]{:S(2)}) %collective-permute-start.1) | collective-permute-done | bytes 1048608 | tf_op jit(solution)/shard_map/ppermute | solution.py:418
  92.8 12.3 %collective-permute-done.5 = bf16[256,1024]{0,1:T(8,128)(2,1)} collective-permute-done((bf16[256,1024]{0,1:T(8,128)(2,1)}, bf16[256,1024]{0,1:T(8,128)(2,1)}, u32[]{:S(2)}, u32[]{:S(2)}) %collective-permute-start.5) | collective-permute-done | bytes 524320 | tf_op jit(solution)/shard_map/ppermute | solution.py:418
  119.6 12.6 %convolution_convert_fusion.6.proj_ref = bf16[2048,896]{1,0:T(8,128)(2,1)S(1)} fusion(bf16[2048,2048]{0,1:T(8,128)(2,1)} %fusion.25, bf16[2048,896]{1,0:T(8,128)(2,1)} %all-gather.5.cloned.1.call-done), kind=kOutput, calls=%fused_computation.17 | convolution fusion | flops 7518027776 | bytes 15728640 | tf_op jit(solution)/shard_map/dot_general | solution.py:19
  137.8 29.8 %delta_forward_one.1 = (f32[2048,768]{1,0:T(8,128)}, bf16[2048,768]{1,0:T(8,128)(2,1)}, f32[2048,128]{1,0:T(8,128)S(1)}, bf16[2,16,128,128]{3,2,1,0:T(8,128)(2,1...) custom-call(s32[1]{0:T(128)} %bitcast.q_ref, bf16[2048,896]{1,0:T(8,128)(2,1)} %copy-done.29, ...), custom_call_target="tpu_custom_call" | custom-call | flops 6710886400 | bytes 17787392 | tf_op jit(solution)/shard_map/delta_forward_one/pallas_call | solution.py:337
  198.1 17.5 %delta_forward_two.1 = (bf16[2048,256]{1,0:T(8,128)(2,1)S(1)}, f32[2048,256]{1,0:T(8,128)}, bf16[2,16,128,128]{3,2,1,0:T(8,128)(2,1)S(1)}, bf16[2,16,128,128]{3,2,1,0:T(8,128)(2,1)S(1)}) custom-call(s32[1]{0:T(128)} %bitcast.q_ref, bf16[2048,768]{1,0:T(8,128)(2,1)} %get-tuple-element.37.qkv_ref, f32[2048,128]{1,0:T(8,128)S(1)} %copy-done.5, ...), custom_call_target="tpu_custom_call" | custom-call | flops 1073741824 | bytes 12911104 | tf_op jit(solution)/shard_map/delta_forward_two/pallas_call | solution.py:337
  235.5 12.2 %collective-permute-done.22 = bf16[256,1024]{0,1:T(8,128)(2,1)S(1)} collective-permute-done((bf16[256,1024]{0,1:T(8,128)(2,1)S(1)}, bf16[256,1024]{0,1:T(8,128)(2,1)S(1)}, u32[]{:S(2)}, u32[]{:S(2)}) %collective-permute-start.22) | collective-permute-done | bytes 524320 | tf_op jit(solution)/shard_map/ppermute | solution.py:418
  259.0 17.9 %collective-permute-done.23 = bf16[512,1024]{0,1:T(8,128)(2,1)} collective-permute-done((bf16[512,1024]{0,1:T(8,128)(2,1)}, bf16[512,1024]{0,1:T(8,128)(2,1)}, u32[]{:S(2)}, u32[]{:S(2)}) %collective-permute-start.23) | collective-permute-done | bytes 1048608 | tf_op jit(solution)/shard_map/ppermute | solution.py:418
  281.9 18.8 %collective-permute-done.47 = bf16[512,1024]{0,1:T(8,128)(2,1)} collective-permute-done((bf16[512,1024]{0,1:T(8,128)(2,1)}, bf16[512,1024]{0,1:T(8,128)(2,1)}, u32[]{:S(2)}, u32[]{:S(2)}) %collective-permute-start.47) | collective-permute-done | bytes 1048608 | tf_op jit(solution)/shard_map/ppermute | solution.py:418
  324.5 26.7 %collective-permute-done.51 = bf16[256,1024]{0,1:T(8,128)(2,1)} collective-permute-done((bf16[256,1024]{0,1:T(8,128)(2,1)}, bf16[256,1024]{0,1:T(8,128)(2,1)}, u32[]{:S(2)}, u32[]{:S(2)}) %collective-permute-start.51) | collective-permute-done | bytes 524320 | tf_op jit(solution)/shard_map/ppermute | solution.py:418
  387.7 19.2 %fusion.113 = f32[2048,1536]{0,1:T(8,128)} fusion(bf16[2048,2048]{0,1:T(8,128)(2,1)} %fusion.27, bf16[2048,1536]{1,0:T(8,128)(2,1)} %all-gather.9.cloned.1.call-done), kind=kOutput, calls=%fused_computation.379 | convolution fusion | flops 12884901888 | bytes 27262976 | tf_op jit(solution)/shard_map/dot_general | solution.py:19
  406.8 17.9 %multiply_convert_fusion.1 = (bf16[2048,768]{0,1:T(8,128)(2,1)}, bf16[2048,768]{0,1:T(8,128)(2,1)}, bf16[2048,768]{0,1:T(8,128)(2,1)}) fusion(f32[2048,1536]{0,1:T(8,128)} %fusion.113, bf16[2048,2048]{0,1:T(8,128)(2,1)} %copy-done.39, bf16[2048,768]{1,0:T(8,128)(2,1)} %all-gather.11.cloned.1.call-done), kind=kOutput, calls=%fused_computation.7 | convolution fusion | flops 6467616768 | bytes 33554432 | tf_op jit(solution)/shard_map/dot_general | solution.py:19
  424.8 11.2 %convolution_convert_fusion.1 = bf16[2048,1024]{0,1:T(8,128)(2,1)} fusion(bf16[2048,1536]{1,0:T(8,128)(2,1)S(1)} %copy-done.53, s32[]{:T(128)S(6)} %select_n.941, bf16[2048,768]{0,1:T(8,128)(2,1)} %get-tuple-element.170, bf16[2048,768]{0,1:T(8,128)(2,1)} %get-tuple-element.169), kind=kOutput, calls=%fused_computation.12 | convolution fusion | flops 6457131008 | bytes 13631492 | tf_op jit(solution)/shard_map/dot_general | solution.py:23
  441.7 10.3 %convolution_convert_fusion.7 = bf16[2048,768]{1,0:T(8,128)(2,1)} fusion(bf16[2048,2048]{0,1:T(8,128)(2,1)} %copy-done.39, bf16[2048,768]{0,1:T(8,128)(2,1)S(1)} %copy-done.59), kind=kOutput, calls=%fused_computation.18 | convolution fusion | flops 6444023808 | bytes 14680064 | tf_op jit(solution)/shard_map/dot_general | solution.py:27
  452.1 10.9 %add_convert_fusion.1 = bf16[2048,1024]{0,1:T(8,128)(2,1)S(1)} fusion(bf16[2048,1024]{0,1:T(8,128)(2,1)} %collective-permute-done.55, bf16[2048,1536]{1,0:T(8,128)(2,1)} %all-gather.9.cloned.1.call-done, s32[]{:T(128)S(6)} %select_n.882, bf16[2048,768]{0,1:T(8,128)(2,1)} %get-tuple-element.170, bf16[2048,768]{0,1:T(8,128)(2,1)} %get-tuple-element.169), kind=kOutput, calls=%fused_computation.1 | convolution fusion | flops 6461325312 | bytes 17825796 | tf_op jit(solution)/shard_map/dot_general | solution.py:23
  492.3 19.9 %collective-permute-done.59 = bf16[512,1024]{0,1:T(8,128)(2,1)S(1)} collective-permute-done((bf16[512,1024]{0,1:T(8,128)(2,1)S(1)}, bf16[512,1024]{0,1:T(8,128)(2,1)S(1)}, u32[]{:S(2)}, u32[]{:S(2)}) %collective-permute-start.59) | collective-permute-done | bytes 1048608 | tf_op jit(solution)/shard_map/ppermute | solution.py:418
  514.4 19.6 %collective-permute-done.44 = bf16[512,1024]{0,1:T(8,128)(2,1)S(1)} collective-permute-done((bf16[512,1024]{0,1:T(8,128)(2,1)S(1)}, bf16[512,1024]{0,1:T(8,128)(2,1)S(1)}, u32[]{:S(2)}, u32[]{:S(2)}) %collective-permute-start.44) | collective-permute-done | bytes 1048608 | tf_op jit(solution)/shard_map/ppermute | solution.py:418
  540.5 22.6 %collective-permute-done.62 = bf16[512,1024]{0,1:T(8,128)(2,1)S(1)} collective-permute-done((bf16[512,1024]{0,1:T(8,128)(2,1)S(1)}, bf16[512,1024]{0,1:T(8,128)(2,1)S(1)}, u32[]{:S(2)}, u32[]{:S(2)}) %collective-permute-start.62) | collective-permute-done | bytes 1048608 | tf_op jit(solution)/shard_map/ppermute | solution.py:418
  566.4 12.3 %collective-permute-done.68 = bf16[256,1024]{0,1:T(8,128)(2,1)S(1)} collective-permute-done((bf16[256,1024]{0,1:T(8,128)(2,1)S(1)}, bf16[256,1024]{0,1:T(8,128)(2,1)S(1)}, u32[]{:S(2)}, u32[]{:S(2)}) %collective-permute-start.68) | collective-permute-done | bytes 524320 | tf_op jit(solution)/shard_map/ppermute | solution.py:418
  588.9 18.7 %convolution_convert_fusion = bf16[2048,1536]{1,0:T(8,128)(2,1)} fusion(bf16[2048,2048]{0,1:T(8,128)(2,1)} %fusion.27, bf16[2048,768]{0,1:T(8,128)(2,1)} %get-tuple-element.170, bf16[2048,768]{0,1:T(8,128)(2,1)} %get-tuple-element.169), kind=kOutput, calls=%fused_computation.4 | convolution fusion | flops 12900630528 | bytes 20971520 | tf_op jit(solution)/shard_map/dot_general | solution.py:27
  615.3 20.3 %delta_backward_one.1 = (bf16[2048,256]{1,0:T(8,128)(2,1)S(1)}, f32[2,16,128,128]{3,2,1,0:T(8,128)}, bf16[2,16,128,128]{3,2,1,0:T(8,128)(2,1)S(1)}, bf16[2,16,12...) custom-call(s32[1]{0:T(128)} %bitcast.q_ref, f32[2048,256]{1,0:T(8,128)} %fusion.114.dout_ref, ...), custom_call_target="tpu_custom_call" | custom-call | flops 1610612736 | bytes 16188416 | tf_op jit(solution)/shard_map/delta_backward_one/pallas_call | solution.py:337
  639.8 13.4 %collective-permute-done.70 = f32[2,128,128]{2,1,0:T(8,128)S(1)} collective-permute-done((f32[2,128,128]{2,1,0:T(8,128)S(1)}, f32[2,128,128]{2,1,0:T(8,128)S(1)}, u32[]{:S(2)}, u32[]{:S(2)}) %collective-permute-start.70) | collective-permute-done | bytes 131104 | tf_op jit(solution)/shard_map/ppermute | solution.py:423
  681.7 24.5 %delta_backward_two.1 = (bf16[2048,896]{1,0:T(8,128)(2,1)}, f32[8,768]{1,0:T(8,128)S(1)}, f32[4,768]{1,0:T(4,128)S(1)}, f32[1,128]{1,0:T(1,128)S(1)}) custom-call(s32[1]{0:T(128)} %bitcast.q_ref, f32[2048,768]{1,0:T(8,128)} %get-tuple-element.43.pre_ref, bf16[2048,896]{1,0:T(8,128)(2,1)} %copy-done.29, f32[4,768]{1,0:T(4,128)S(1)} %pad_maximum_fusion.20.taps_ref, ...), custom_call_target="tpu_custom_call" | custom-call | flops 1879048192 | bytes 26591744 | tf_op jit(solution)/shard_map/delta_backward_two/pallas_call | solution.py:337
  744.1 13.6 %convolution_convert_fusion.5 = bf16[2048,896]{1,0:T(8,128)(2,1)} fusion(bf16[2048,2048]{0,1:T(8,128)(2,1)} %fusion.25, bf16[2048,896]{1,0:T(8,128)(2,1)} %constant_dynamic-update-slice_fusion.1), kind=kOutput, calls=%fused_computation.16 | convolution fusion | flops 7518027776 | bytes 15728640 | tf_op jit(solution)/shard_map/dot_general | solution.py:27
  817.9 15.3 %collective-permute-done.78 = bf16[512,1024]{0,1:T(8,128)(2,1)S(1)} collective-permute-done((bf16[512,1024]{0,1:T(8,128)(2,1)S(1)}, bf16[512,1024]{0,1:T(8,128)(2,1)S(1)}, u32[]{:S(2)}, u32[]{:S(2)}) %collective-permute-start.78) | collective-permute-done | bytes 1048608 | tf_op jit(solution)/shard_map/ppermute | solution.py:418
  (543 shorter events, 473.0 us)
Async XLA Ops:
  7.2 112.4 %all-gather.5.cloned.1.call-start = ((), (), s32[]{:S(2)}) async-start(), calls=%async_computation.4 | async-start | bytes 4587520 | tf_op jit(solution)/shard_map/all_gather | solution.py:578
  28.5 189.1 %all-gather.7.cloned.1.call-start = ((), (), s32[]{:S(2)}) async-start(), calls=%async_computation.5 | async-start | bytes 1310720 | tf_op jit(solution)/shard_map/all_gather | solution.py:578
  42.4 44.9 %collective-permute-start = (bf16[512,1024]{0,1:T(8,128)(2,1)}, bf16[512,1024]{0,1:T(8,128)(2,1)}, u32[]{:S(2)}, u32[]{:S(2)}) collective-permute-start(bf16[512,1024]{0,1:T(8,128)(2,1)} %multiply_convert_fusion.4), channel_id=1, source_target_pairs={{0,1},{1,0},{2,3},{3,2},{4,5},{5,4},{6,7},{7,6},{8,9},{9,8},{10,11... | collective-permute-start | bytes 3145736 | tf_op jit(solution)/shard_map/ppermute | solution.py:418
  47.6 34.5 %collective-permute-start.17 = (bf16[128,256]{1,0:T(8,128)(2,1)}, bf16[128,256]{1,0:T(8,128)(2,1)}, u32[]{:S(2)}, u32[]{:S(2)}) collective-permute-start(bf16[128,256]{1,0:T(8,128)(2,1)} %bitcast.16), channel_id=1, source_target_pairs={{0,4},{4,0},{1,5},{5,1},{2,6},{6,2},{3,7},{7,3},{8,12},{12,8},{9,1... | collective-permute-start | bytes 196616 | tf_op jit(solution)/shard_map/ppermute | solution.py:418
  67.2 38.5 %collective-permute-start.2 = (bf16[512,1024]{0,1:T(8,128)(2,1)}, bf16[512,1024]{0,1:T(8,128)(2,1)}, u32[]{:S(2)}, u32[]{:S(2)}) collective-permute-start(bf16[512,1024]{0,1:T(8,128)(2,1)} %collective-permute-done.1), channel_id=1, source_target_pairs={{0,1},{1,0},{2,3},{3,2},{4,5},{5,4},{6,7},{7,6},{8,9},{9,8},{10,11... | collective-permute-start | bytes 3145736 | tf_op jit(solution)/shard_map/ppermute | solution.py:418
  70.2 41.1 %collective-permute-start.4 = (bf16[512,1024]{0,1:T(8,128)(2,1)}, bf16[512,1024]{0,1:T(8,128)(2,1)}, u32[]{:S(2)}, u32[]{:S(2)}) collective-permute-start(bf16[512,1024]{0,1:T(8,128)(2,1)} %collective-permute-done.3), channel_id=1, source_target_pairs={{0,1},{1,0},{2,3},{3,2},{4,5},{5,4},{6,7},{7,6},{8,9},{9,8},{10,11... | collective-permute-start | bytes 3145736 | tf_op jit(solution)/shard_map/ppermute | solution.py:418
  82.1 53.6 %collective-permute-start.34 = (bf16[128,1536]{1,0:T(8,128)(2,1)}, bf16[128,1536]{1,0:T(8,128)(2,1)}, u32[]{:S(2)}, u32[]{:S(2)}) collective-permute-start(bf16[128,1536]{1,0:T(8,128)(2,1)} %pad_maximum_fusion.15), channel_id=1, source_target_pairs={{0,6},{2,4},{4,2},{6,0},{1,7},{3,5},{5,3},{7,1},{8,14},{10,12},{12... | collective-permute-start | bytes 1179656 | tf_op jit(solution)/shard_map/ppermute | solution.py:418
  86.0 301.6 %all-gather.9.cloned.1.call-start = ((), (), s32[]{:S(2)}) async-start(), calls=%async_computation.6 | async-start | bytes 7864320 | tf_op jit(solution)/shard_map/all_gather | solution.py:578
  175.9 230.9 %all-gather.11.cloned.1.call-start = ((), (), s32[]{:S(2)}) async-start(), calls=%async_computation.7 | async-start | bytes 3932160 | tf_op jit(solution)/shard_map/all_gather | solution.py:578
  255.5 45.2 %collective-permute-start.47 = (bf16[512,1024]{0,1:T(8,128)(2,1)}, bf16[512,1024]{0,1:T(8,128)(2,1)}, u32[]{:S(2)}, u32[]{:S(2)}) collective-permute-start(bf16[512,1024]{0,1:T(8,128)(2,1)} %copy.202), channel_id=1, source_target_pairs={{0,2},{2,0},{1,3},{3,1},{4,6},{6,4},{5,7},{7,5},{8,10},{10,8},{9,1... | collective-permute-start | bytes 3145736 | tf_op jit(solution)/shard_map/ppermute | solution.py:418
  257.3 56.7 %collective-permute-start.49 = (bf16[512,1024]{0,1:T(8,128)(2,1)}, bf16[512,1024]{0,1:T(8,128)(2,1)}, u32[]{:S(2)}, u32[]{:S(2)}) collective-permute-start(bf16[512,1024]{0,1:T(8,128)(2,1)} %copy.202), channel_id=1, source_target_pairs={{0,4},{4,0},{1,5},{5,1},{2,6},{6,2},{3,7},{7,3},{8,12},{12,8},{9,1... | collective-permute-start | bytes 3145736 | tf_op jit(solution)/shard_map/ppermute | solution.py:418
  259.0 57.7 %collective-permute-start.46 = (bf16[512,1024]{0,1:T(8,128)(2,1)}, bf16[512,1024]{0,1:T(8,128)(2,1)S(1)}, u32[]{:S(2)}, u32[]{:S(2)}) collective-permute-start(bf16[512,1024]{0,1:T(8,128)(2,1)} %copy.202), channel_id=1, source_target_pairs={{0,1},{1,0},{2,3},{3,2},{4,5},{5,4},{6,7},{7,6},{8,9},{9,8},{10,11... | collective-permute-start | bytes 3145736 | tf_op jit(solution)/shard_map/ppermute | solution.py:418
  312.8 38.4 %collective-permute-start.48 = (bf16[512,1024]{0,1:T(8,128)(2,1)}, bf16[512,1024]{0,1:T(8,128)(2,1)}, u32[]{:S(2)}, u32[]{:S(2)}) collective-permute-start(bf16[512,1024]{0,1:T(8,128)(2,1)} %collective-permute-done.47), channel_id=1, source_target_pairs={{0,1},{1,0},{2,3},{3,2},{4,5},{5,4},{6,7},{7,6},{8,9},{9,8},{10,11... | collective-permute-start | bytes 3145736 | tf_op jit(solution)/shard_map/ppermute | solution.py:418
  314.0 40.6 %collective-permute-start.50 = (bf16[512,1024]{0,1:T(8,128)(2,1)}, bf16[512,1024]{0,1:T(8,128)(2,1)}, u32[]{:S(2)}, u32[]{:S(2)}) collective-permute-start(bf16[512,1024]{0,1:T(8,128)(2,1)} %collective-permute-done.49), channel_id=1, source_target_pairs={{0,1},{1,0},{2,3},{3,2},{4,5},{5,4},{6,7},{7,6},{8,9},{9,8},{10,11... | collective-permute-start | bytes 3145736 | tf_op jit(solution)/shard_map/ppermute | solution.py:418
  314.5 40.1 %collective-permute-start.26 = (bf16[512,1024]{0,1:T(8,128)(2,1)}, bf16[512,1024]{0,1:T(8,128)(2,1)}, u32[]{:S(2)}, u32[]{:S(2)}) collective-permute-start(bf16[512,1024]{0,1:T(8,128)(2,1)} %multiply_convert_fusion.3), channel_id=1, source_target_pairs={{0,2},{2,0},{1,3},{3,1},{4,6},{6,4},{5,7},{7,5},{8,10},{10,8},{9,1... | collective-permute-start | bytes 3145736 | tf_op jit(solution)/shard_map/ppermute | solution.py:418
  316.7 34.4 %collective-permute-start.51 = (bf16[256,1024]{0,1:T(8,128)(2,1)}, bf16[256,1024]{0,1:T(8,128)(2,1)}, u32[]{:S(2)}, u32[]{:S(2)}) collective-permute-start(bf16[256,1024]{0,1:T(8,128)(2,1)} %slice.418), channel_id=1, source_target_pairs={{0,2},{2,0},{1,3},{3,1},{4,6},{6,4},{5,7},{7,5},{8,10},{10,8},{9,1... | collective-permute-start | bytes 1572872 | tf_op jit(solution)/shard_map/ppermute | solution.py:418
  319.3 38.9 %collective-permute-start.28 = (bf16[512,1024]{0,1:T(8,128)(2,1)}, bf16[512,1024]{0,1:T(8,128)(2,1)}, u32[]{:S(2)}, u32[]{:S(2)}) collective-permute-start(bf16[512,1024]{0,1:T(8,128)(2,1)} %multiply_convert_fusion.3), channel_id=1, source_target_pairs={{0,4},{4,0},{1,5},{5,1},{2,6},{6,2},{3,7},{7,3},{8,12},{12,8},{9,1... | collective-permute-start | bytes 3145736 | tf_op jit(solution)/shard_map/ppermute | solution.py:418
  321.6 405.6 %reduce-scatter.11.cloned.1.call-start = ((), (), s32[]{:S(2)}) async-start(), calls=%async_computation.11 | async-start | bytes 3932160 | tf_op jit(solution)/shard_map/reduce_scatter | solution.py:644
  452.0 313.3 %reduce-scatter.7.cloned.1.call-start = ((), (), s32[]{:S(2)}) async-start(), calls=%async_computation.9 | async-start | bytes 1310720 | tf_op jit(solution)/shard_map/reduce_scatter | solution.py:644
  490.1 43.8 %collective-permute-start.44 = (bf16[512,1024]{0,1:T(8,128)(2,1)S(1)}, bf16[512,1024]{0,1:T(8,128)(2,1)S(1)}, u32[]{:S(2)}, u32[]{:S(2)}) collective-permute-start(bf16[512,1024]{0,1:T(8,128)(2,1)S(1)} %pad_maximum_fusion.8), channel_id=1, source_target_pairs={{0,4},{4,0},{1,5},{5,1},{2,6},{6,2},{3,7},{7,3},{8,12},{12,8},{9,1... | collective-permute-start | bytes 3145736 | tf_op jit(solution)/shard_map/ppermute | solution.py:418
  490.6 43.4 %collective-permute-start.42 = (bf16[512,1024]{0,1:T(8,128)(2,1)S(1)}, bf16[512,1024]{0,1:T(8,128)(2,1)S(1)}, u32[]{:S(2)}, u32[]{:S(2)}) collective-permute-start(bf16[512,1024]{0,1:T(8,128)(2,1)S(1)} %pad_maximum_fusion.7), channel_id=1, source_target_pairs={{0,2},{2,0},{1,3},{3,1},{4,6},{6,4},{5,7},{7,5},{8,10},{10,8},{9,1... | collective-permute-start | bytes 3145736 | tf_op jit(solution)/shard_map/ppermute | solution.py:418
  588.8 196.5 %reduce-scatter.9.cloned.1.call-start = ((), (), s32[]{:S(2)}) async-start(), calls=%async_computation.10 | async-start | bytes 7864320 | tf_op jit(solution)/shard_map/reduce_scatter | solution.py:644
  607.6 249.8 %reduce-scatter.5.cloned.1.call-start = ((), (), s32[]{:S(2)}) async-start(), calls=%async_computation.8 | async-start | bytes 4587520 | tf_op jit(solution)/shard_map/reduce_scatter | solution.py:644
  727.3 42.5 %collective-permute-start.74 = (bf16[2048,1024]{0,1:T(8,128)(2,1)}, bf16[2048,1024]{0,1:T(8,128)(2,1)}, u32[]{:S(2)}, u32[]{:S(2)}) collective-permute-start(bf16[2048,1024]{0,1:T(8,128)(2,1)} %convolution_convert_fusion.4), channel_id=1, source_target_pairs={{0,1},{1,0},{2,3},{3,2},{4,5},{5,4},{6,7},{7,6},{8,9},{9,8},{10,11... | collective-permute-start | bytes 12582920 | tf_op jit(solution)/shard_map/ppermute | solution.py:418
  (143 other events, 2292.1 us)
Sparse Core Ops, SparseCore 0:
  28.6 69.9 all-gather.4
  100.1 28.8 all-gather.6
  176.0 114.7 all-gather.8
  321.7 61.4 all-gather.10
  452.1 59.9 reduce-scatter.10
  588.9 25.6 reduce-scatter.6
  617.0 120.4 reduce-scatter.8
  757.8 67.3 reduce-scatter.4
